TPU v7x, 32 devices: a whole 2x2x4 slice. The times are simulated.
32 devices in a mesh: groups: 2 (over x), grid: 4 (over y, core), rep: 4 (over z).
Axes of the slice: x: 2, y: 2, z: 4, core: 2. Of those that a mesh axis runs over, the one named last changes fastest.
Arguments:
- x_vals: bfloat16 [512, 6, 128, 128], P(('groups', 'grid', 'rep')), parts along dimension 0, may hold values from -6 to 6
- x_cols: int32 [512, 6], P('groups'), parts along dimension 0, may hold values from 0 to 255, as said below
- p_cols: int32 [512, 10], P('groups'), parts along dimension 0, may hold values from 0 to 255, as said below
Outputs:
- new_vals: bfloat16 [512, 10, 128, 128], P(('groups', 'grid', 'rep')), parts along dimension 0
There are 2 independent parts, one for each index of `groups`. A program takes and returns all parts, laid end to end along the dimension named above; each array names one. Nothing has to cross between parts.
Inputs may be any that keep to these rules, and one draw needn't show every extreme that they name: `x_cols`: block row i lists 6 different block columns (i + d) mod 256 with -4 <= d <= 4, d = 0 among them, ordered by increasing d. `p_cols`: block row i lists 10 different block columns (i + d) mod 256 with -8 <= d <= 8, d = 0 among them, ordered by increasing d.
All inputs are finite; a program needn't handle non-finite values.
Results may differ from a plain program's by a relative error of at most 0.0013.
Values may be sent and summed in bfloat16 or wider, within the bound.
No kernel may reach another device: no remote copies, remote signals or barrier semaphores. Data moves between devices by JAX's collectives and lax.ppermute only.
A program may use at most 64 MiB of HBM per device.

v0:
```python
from functools import partial

import jax
import jax.numpy as jnp
from jax import lax
from jax.sharding import PartitionSpec as P

BAND = 4


def extended(block, sides, width):
    for axis, dim in sides:
        count = lax.axis_size(axis)
        forward = [(i, i + 1) for i in range(count - 1)]
        forward.append((count - 1, 0))
        backward = [(target, source) for source, target in forward]
        low = lax.ppermute(
            lax.slice_in_dim(block, block.shape[dim] - width, None, axis=dim), axis, forward
        )
        high = lax.ppermute(lax.slice_in_dim(block, 0, width, axis=dim), axis, backward)
        block = jnp.concatenate([low, block, high], axis=dim)
    return block


def body(x_vals, x_cols, p_cols):
    row_count = x_vals.shape[0]
    slot_count = x_vals.shape[1]
    block_size = x_vals.shape[2]
    total_blocks = x_cols.shape[0]
    first_row = lax.axis_index(("grid", "rep")) * row_count
    gram_scale = 1.0 / (4 * slot_count * block_size)

    def pick_blocks(source_rows, centre, natural_row, cols_of_rows, wanted):
        neighbour_rows = x_cols[natural_row]
        distance = (neighbour_rows - natural_row + BAND) % total_blocks - BAND
        far_blocks = jnp.take(source_rows, centre + distance, axis=0)
        select = (cols_of_rows[neighbour_rows][:, :, None] == wanted[None, None, :]).astype(
            jnp.bfloat16
        )
        chosen = jnp.einsum(
            "akzy,akp->apzy", far_blocks, select, preferred_element_type=jnp.float32
        )
        return chosen.astype(jnp.bfloat16)

    def gram_block_row(padded, margin, local_row):
        natural_row = (first_row + local_row) % total_blocks
        own_blocks = lax.dynamic_index_in_dim(padded, local_row + margin, 0, keepdims=False)
        chosen = pick_blocks(padded, local_row + margin, natural_row, x_cols, p_cols[natural_row])
        summed = jnp.einsum("axz,apzy->pxy", own_blocks, chosen, preferred_element_type=jnp.float32)
        return (summed * gram_scale).astype(jnp.bfloat16)

    padded = extended(x_vals, ((("grid", "rep"), 0),), BAND)
    own_rows = jnp.arange(row_count, dtype=jnp.int32)
    gram_rows = lax.map(partial(gram_block_row, padded, BAND), own_rows)
    gram_padded = extended(gram_rows, ((("grid", "rep"), 0),), BAND)

    def update_block_row(local_row):
        natural_row = (first_row + local_row) % total_blocks
        own_blocks = x_vals[local_row]
        wanted = p_cols[natural_row]
        chosen = pick_blocks(gram_padded, local_row + BAND, natural_row, p_cols, wanted)
        carried = jnp.einsum(
            "axz,apzy->pxy", own_blocks, chosen, preferred_element_type=jnp.float32
        )
        present = (x_cols[natural_row][:, None] == wanted[None, :]).astype(jnp.bfloat16)
        kept = jnp.einsum("bp,bxy->pxy", present, own_blocks, preferred_element_type=jnp.float32)
        return (1.5 * kept - 0.5 * carried).astype(jnp.bfloat16)

    return lax.map(update_block_row, jnp.arange(row_count, dtype=jnp.int32))


def solution(mesh):
    return jax.shard_map(
        body,
        mesh=mesh,
        in_specs=(
            P(("groups", "grid", "rep"), None, None, None),
            P("groups", None),
            P("groups", None),
        ),
        out_specs=P(("groups", "grid", "rep"), None, None, None),
        check_vma=False,
    )
```

profile of v0, /device:TPU:0, one launch (start us, length us, event | category | flops | bytes accessed | tf_op | source)
XLA Modules:
  0.0 786.9 jit_solution(4119461784506026312)
XLA Ops:
  8.6 17.5 %collective-permute-done = bf16[4,6,128,128]{3,2,1,0:T(8,128)(2,1)} collective-permute-done((bf16[4,6,128,128]{3,2,1,0:T(8,128)(2,1)}, bf16[4,6,128,128]{3,2,1,0:T(8,128)(2,1)}, u32[]{:S(2)}, u32[]{:S(2)}) %collective-permute-start) | collective-permute-done | bytes 786464 | tf_op jit(solution)/shard_map/ppermute | solution.py:17
  26.0 16.0 %collective-permute-done.1 = bf16[4,6,128,128]{3,2,1,0:T(8,128)(2,1)} collective-permute-done((bf16[4,6,128,128]{3,2,1,0:T(8,128)(2,1)}, bf16[4,6,128,128]{3,2,1,0:T(8,128)(2,1)}, u32[]{:S(2)}, u32[]{:S(2)}) %collective-permute-start.1) | collective-permute-done | bytes 786464 | tf_op jit(solution)/shard_map/ppermute | solution.py:20
  42.1 3.5 pad_maximum_fusion.1
  45.6 3.7 broadcast.452.clone2
  49.3 270.0 %while.24 = (s32[]{:T(128)}, bf16[16,10,128,128]{3,2,1,0:T(8,128)(2,1)}, s32[16]{0:T(128)S(1)}, s32[]{:T(128)}, s32[256,6]{1,0:T(8,128)S(1)}, /*index=5*/s32[256...) while((s32[]{:T(128)}, ...), condition=%wide.region_1.2_spmd, body=%wide.region_0.1_spmd.sunk | while | flops 264374912 | bytes 15607398 | solution.py:54
  325.7 29.4 %collective-permute-done.2 = bf16[4,10,128,128]{3,2,1,0:T(8,128)(2,1)} collective-permute-done((bf16[4,10,128,128]{3,2,1,0:T(8,128)(2,1)S(1)}, bf16[4,10,128,128]{3,2,1,0:T(8,128)(2,1)}, u32[]{:S(2)}, u32[]{:S(2)}) %collective-permute-start.2) | collective-permute-done | bytes 1310752 | tf_op jit(solution)/shard_map/ppermute | solution.py:17
  355.0 25.9 %collective-permute-done.3 = bf16[4,10,128,128]{3,2,1,0:T(8,128)(2,1)} collective-permute-done((bf16[4,10,128,128]{3,2,1,0:T(8,128)(2,1)S(1)}, bf16[4,10,128,128]{3,2,1,0:T(8,128)(2,1)}, u32[]{:S(2)}, u32[]{:S(2)}) %collective-permute-start.3) | collective-permute-done | bytes 1310752 | tf_op jit(solution)/shard_map/ppermute | solution.py:20
  380.9 6.9 pad_maximum_fusion
  387.9 3.7 broadcast.452.clone
  391.5 395.3 %while.25 = (s32[]{:T(128)}, bf16[16,10,128,128]{3,2,1,0:T(8,128)(2,1)}, s32[16]{0:T(128)S(1)}, s32[]{:T(128)}, s32[256,6]{1,0:T(8,128)S(1)}, /*index=5*/s32[256...) while((s32[]{:T(128)}, ...), condition=%wide.region_3.4_spmd, body=%wide.region_2.3_spmd.sunk | while | flops 274926496 | bytes 22751224 | solution.py:69
  393.6 5.5 gather_fusion.2
  404.9 3.9 copy.60
  418.3 5.5 gather_fusion.2
  429.6 3.9 copy.60
  443.0 5.5 gather_fusion.2
  450.9 3.4 fusion.114
  454.3 3.9 copy.60
  467.7 5.5 gather_fusion.2
  479.0 3.9 copy.60
  492.5 5.5 gather_fusion.2
  503.8 3.9 copy.60
  517.2 5.5 gather_fusion.2
  525.0 3.4 fusion.114
  528.5 3.9 copy.60
  541.9 5.5 gather_fusion.2
  553.2 3.9 copy.60
  566.6 5.5 gather_fusion.2
  574.4 3.4 fusion.114
  577.9 3.9 copy.60
  591.3 5.5 gather_fusion.2
  602.6 3.9 copy.60
  616.0 5.5 gather_fusion.2
  623.9 3.4 fusion.114
  627.3 3.9 copy.60
  640.7 5.5 gather_fusion.2
  652.0 3.9 copy.60
  665.4 5.5 gather_fusion.2
  676.7 3.9 copy.60
  690.1 5.5 gather_fusion.2
  698.0 3.4 fusion.114
  701.4 3.9 copy.60
  714.8 5.5 gather_fusion.2
  726.1 3.9 copy.60
  739.5 5.5 gather_fusion.2
  747.4 3.4 fusion.114
  750.8 3.9 copy.60
  764.2 5.5 gather_fusion.2
  775.5 3.9 copy.60
  (474 shorter events, 422.3 us)
Async XLA Ops:
  0.0 42.1 %copy-start = (bf16[16,6,128,128]{3,2,1,0:T(8,128)(2,1)S(1)}, bf16[16,6,128,128]{3,2,1,0:T(8,128)(2,1)}, u32[]{:S(2)}) copy-start(bf16[16,6,128,128]{3,2,1,0:T(8,128)(2,1)} %param.7) | copy-start | bytes 9437188
  0.0 8.3 %copy-start.2 = (s32[256,6]{0,1:T(8,128)S(1)}, s32[256,6]{0,1:T(8,128)}, u32[]{:S(2)}) copy-start(s32[256,6]{0,1:T(8,128)} %param.8) | copy-start | bytes 18436
  0.0 8.5 %copy-start.1 = (s32[256,10]{0,1:T(8,128)S(1)}, s32[256,10]{0,1:T(8,128)}, u32[]{:S(2)}) copy-start(s32[256,10]{0,1:T(8,128)} %param.9) | copy-start | bytes 30724
  2.9 23.2 %collective-permute-start = (bf16[4,6,128,128]{3,2,1,0:T(8,128)(2,1)}, bf16[4,6,128,128]{3,2,1,0:T(8,128)(2,1)}, u32[]{:S(2)}, u32[]{:S(2)}) collective-permute-start(bf16[4,6,128,128]{3,2,1,0:T(8,128)(2,1)} %get-tuple-element.270), channel_id=1, source_target_pairs={{0,1},{1,2},{2,3},{3,4},{4,5},{5,6},{6,7},{7,8},{8,9},{9,10},{10,1... | collective-permute-start | bytes 2359304 | tf_op jit(solution)/shard_map/ppermute | solution.py:17
  5.9 36.2 %collective-permute-start.1 = (bf16[4,6,128,128]{3,2,1,0:T(8,128)(2,1)}, bf16[4,6,128,128]{3,2,1,0:T(8,128)(2,1)}, u32[]{:S(2)}, u32[]{:S(2)}) collective-permute-start(bf16[4,6,128,128]{3,2,1,0:T(8,128)(2,1)} %get-tuple-element.271), channel_id=1, source_target_pairs={{1,0},{2,1},{3,2},{4,3},{5,4},{6,5},{7,6},{8,7},{9,8},{10,9},{11,1... | collective-permute-start | bytes 2359304 | tf_op jit(solution)/shard_map/ppermute | solution.py:20
  321.2 33.9 %collective-permute-start.2 = (bf16[4,10,128,128]{3,2,1,0:T(8,128)(2,1)S(1)}, bf16[4,10,128,128]{3,2,1,0:T(8,128)(2,1)}, u32[]{:S(2)}, u32[]{:S(2)}) collective-permute-start(bf16[4,10,128,128]{3,2,1,0:T(8,128)(2,1)S(1)} %get-tuple-element.268), channel_id=1, source_target_pairs={{0,1},{1,2},{2,3},{3,4},{4,5},{5,6},{6,7},{7,8},{8,9},{9,10},{10,1... | collective-permute-start | bytes 3932168 | tf_op jit(solution)/shard_map/ppermute | solution.py:17
  322.8 58.1 %collective-permute-start.3 = (bf16[4,10,128,128]{3,2,1,0:T(8,128)(2,1)S(1)}, bf16[4,10,128,128]{3,2,1,0:T(8,128)(2,1)}, u32[]{:S(2)}, u32[]{:S(2)}) collective-permute-start(bf16[4,10,128,128]{3,2,1,0:T(8,128)(2,1)S(1)} %get-tuple-element.269), channel_id=1, source_target_pairs={{1,0},{2,1},{3,2},{4,3},{5,4},{6,5},{7,6},{8,7},{9,8},{10,9},{11,1... | collective-permute-start | bytes 3932168 | tf_op jit(solution)/shard_map/ppermute | solution.py:20
where the time goes:
time: 793 us; the launch traced here: 787 us
  local copies, waits for them, and re-layouts  368 us (46%)
  matrix products  172 us (22%)
  waiting for transfers between devices  88.8 us (11%)
  loops' own time  87.5 us (11%)
  other arithmetic  60.7 us (8%)
  starting transfers between devices  9.95 us (1%)
    gather x32, local copies, waits for them, and re-layouts, pick_blocks(): far_blocks = jnp.take(source_rows, centre + distance, axis=0)  137 us
    dot_general x32, local copies, waits for them, and re-layouts, pick_blocks(): jnp.einsum('akzy,akp->apzy', far_blocks, select, preferred_element_type=j...  115 us
    dot_general x32, matrix products, pick_blocks(): jnp.einsum('akzy,akp->apzy', far_blocks, select, preferred_element_type=j...  101 us
    another operation x1, loops' own time, body(): return lax.map(update_block_row, jnp.arange(row_count, dtype=jnp.int32))  55.7 us
    select_n x48, other arithmetic, pick_blocks(): far_blocks = jnp.take(source_rows, centre + distance, axis=0)  48.7 us
    ppermute x2, waiting for transfers between devices, extended(): lax.ppermute(lax.slice_in_dim(block, block.shape[dim] - width, None, axis...  46.8 us
    ppermute x2, waiting for transfers between devices, extended(): lax.ppermute(lax.slice_in_dim(block, 0, width, axis=dim), axis, backward)  41.9 us
    dot_general x16, matrix products, gram_block_row(): jnp.einsum('axz,apzy->pxy', own_blocks, chosen, preferred_element_type=jn...  35.6 us
  transfers between devices with their start and end apart: 4, of which 4 were waited for; matrix products, arithmetic and copies ran while one was open for 0% of the time, Pallas kernels for 0%

commit v1 on v0

v1 whole, which is shorter than its diff:
```python
from functools import partial

import jax
import jax.numpy as jnp
from jax import lax
from jax.experimental import pallas as pl
from jax.experimental.pallas import tpu as pltpu
from jax.sharding import PartitionSpec as P

BAND = 4
REACH = 2 * BAND
AXES = ("grid", "rep")
MIB = 1024 * 1024


def slot_tables(cols, first_row, row_count, reach, width):
    total, slots = cols.shape
    natural = jnp.arange(total, dtype=jnp.int32)[:, None]
    offsets = (cols - natural + reach) % total - reach
    wrapped = jnp.concatenate([offsets[-REACH:], offsets, offsets[:REACH]], axis=0)
    rows = row_count + 2 * REACH
    local = lax.dynamic_slice_in_dim(wrapped, first_row, rows, axis=0)
    zero = rows * slots
    number = jnp.arange(zero, dtype=jnp.int32).reshape(rows, slots, 1) - zero
    place = jnp.arange(32, dtype=jnp.int32) - width
    table = zero + jnp.sum(jnp.where(local[:, :, None] == place, number, 0), axis=1)
    return local, table.astype(jnp.int32)


def row_product(left, right, right_index, left_blocks, slots, wanted):
    own = jnp.concatenate([left[left_blocks[s]] for s in slots], axis=1)
    sums = []
    for p in range(0, wanted, 2):
        columns = [
            jnp.concatenate([right[right_index(s, q)] for s in slots], axis=0)
            for q in (p, p + 1)
        ]
        sums.append(
            jnp.dot(own, jnp.concatenate(columns, axis=1), preferred_element_type=jnp.float32)
        )
    return sums


def gram_row(r, dx, dp, tx, pool, gram, scale):
    nnz, pnz = dx.shape[1], dp.shape[1]
    shift = [dx[r, s] for s in range(nnz)]
    want = [dp[r, p] + 3 * BAND for p in range(pnz)]
    sums = row_product(
        pool, pool, lambda s, p: tx[r + shift[s], want[p] - shift[s]],
        [r * nnz + s for s in range(nnz)], range(nnz), pnz,
    )
    for q, pair in enumerate(sums):
        scaled = (pair * scale).astype(jnp.bfloat16)
        size = scaled.shape[0]
        gram[r * pnz + 2 * q] = scaled[:, :size]
        gram[r * pnz + 2 * q + 1] = scaled[:, size:]


def update_sums(r, slots, dx, dp, tg, pool, gram):
    nnz, pnz = dx.shape[1], dp.shape[1]
    shift = {s: dx[r, s] for s in slots}
    want = [dp[r, p] + 3 * BAND for p in range(pnz)]
    return row_product(
        pool, gram, lambda s, p: tg[r + shift[s], want[p] - shift[s]],
        {s: r * nnz + s for s in slots}, slots, pnz,
    )


def first_kernel(scale, dx, dp, tx, tg, x, low, high, out, part, pool, gram, done, sems):
    nnz, pnz = dx.shape[1], dp.shape[1]
    own = x.shape[0]
    near = low.shape[0]
    rows = own // nnz
    start = REACH * nnz
    copies = [
        pltpu.make_async_copy(x, pool.at[pl.ds(start, own)], sems.at[0]),
        pltpu.make_async_copy(low, pool.at[pl.ds(start - near, near)], sems.at[1]),
        pltpu.make_async_copy(high, pool.at[pl.ds(start + own, near)], sems.at[2]),
    ]
    for copy in copies:
        copy.start()
    pool[pool.shape[0] - 1] = jnp.zeros(pool.shape[1:], pool.dtype)
    gram[gram.shape[0] - 1] = jnp.zeros(gram.shape[1:], gram.dtype)
    for copy in copies:
        copy.wait()

    @pl.loop(REACH, REACH + rows)
    def _(r):
        gram_row(r, dx, dp, tx, pool, gram, scale)

    def update(r, store):
        sums = update_sums(r, range(nnz), dx, dp, tg, pool, gram)
        for p in range(pnz):
            size = pool.shape[1]
            half = sums[p // 2][:, (p % 2) * size:(p % 2 + 1) * size]
            kept = pool[tx[r, dp[r, p] + 3 * BAND]].astype(jnp.float32)
            store(p, 1.5 * kept - 0.5 * half)

    @pl.loop(BAND, rows - BAND)
    def _(i):
        def store(p, value):
            done[(i - BAND) * pnz + p] = value.astype(done.dtype)

        update(REACH + i, store)

    copy = pltpu.make_async_copy(
        done, out.at[pl.ds(BAND * pnz, (rows - 2 * BAND) * pnz)], sems.at[3]
    )
    copy.start()

    @pl.loop(0, 2 * BAND)
    def _(e):
        def store(p, value):
            part[e * pnz + p] = value

        update(REACH + jnp.where(e < BAND, e, rows - 2 * BAND + e), store)

    copy.wait()


def second_kernel(
    scale, dx, dp, tx, tg, x, low, high, far_low, far_high, part, unused, out, pool, gram, sums, done, sems
):
    nnz, pnz = dx.shape[1], dp.shape[1]
    own = x.shape[0]
    near = low.shape[0]
    rows = own // nnz
    start = REACH * nnz
    moves = [
        (x.at[pl.ds(0, near)], start),
        (x.at[pl.ds(own - near, near)], start + own - near),
        (low, start - near),
        (high, start + own),
        (far_low, start - 2 * near),
        (far_high, start + own + near),
    ]
    copies = [
        pltpu.make_async_copy(source, pool.at[pl.ds(place, near)], sems.at[n])
        for n, (source, place) in enumerate(moves)
    ]
    for copy in copies:
        copy.start()
    late = pltpu.make_async_copy(part, sums, sems.at[len(moves)])
    late.start()
    pool[pool.shape[0] - 1] = jnp.zeros(pool.shape[1:], pool.dtype)
    gram[gram.shape[0] - 1] = jnp.zeros(gram.shape[1:], gram.dtype)
    for copy in copies:
        copy.wait()

    @pl.loop(0, 2 * BAND)
    def _(e):
        r = jnp.where(e < BAND, REACH - BAND + e, REACH + rows - BAND + e)
        gram_row(r, dx, dp, tx, pool, gram, scale)

    late.wait()
    outgoing = []
    for e in range(2 * BAND):
        if e < BAND:
            i, slots = e, range(0, BAND - e)
        else:
            i, slots = rows - 2 * BAND + e, range(nnz - 1 - (e - BAND), nnz)
        found = update_sums(REACH + i, slots, dx, dp, tg, pool, gram)
        for p in range(pnz):
            size = pool.shape[1]
            half = found[p // 2][:, (p % 2) * size:(p % 2 + 1) * size]
            done[e * pnz + p] = (sums[e * pnz + p] - 0.5 * half).astype(done.dtype)
        copy = pltpu.make_async_copy(
            done.at[pl.ds(e * pnz, pnz)], out.at[pl.ds(i * pnz, pnz)], sems.at[len(moves) + 1 + e]
        )
        copy.start()
        outgoing.append(copy)
    for copy in outgoing:
        copy.wait()


def body(x_vals, x_cols, p_cols):
    rows, nnz, size, _ = x_vals.shape
    pnz = p_cols.shape[1]
    count = lax.axis_size(AXES)
    first_row = lax.axis_index(AXES) * rows
    scale = 1.0 / (4 * nnz * size)
    padded = rows + 2 * REACH
    forward = [(i, (i + 1) % count) for i in range(count)]
    backward = [(target, source) for source, target in forward]

    x = x_vals.reshape(rows * nnz, size, size)
    near = BAND * nnz
    low = lax.ppermute(x[rows * nnz - near:], AXES, forward)
    high = lax.ppermute(x[:near], AXES, backward)
    far_low = lax.ppermute(x[rows * nnz - 2 * near:rows * nnz - near], AXES, forward)
    far_high = lax.ppermute(x[near:2 * near], AXES, backward)

    dx, tx = slot_tables(x_cols, first_row, rows, BAND, 3 * BAND)
    dp, tg = slot_tables(p_cols, first_row, rows, REACH, 3 * BAND)
    row = jnp.arange(padded)[:, None]
    mine = (row >= REACH) & (row < REACH + rows)
    tg_own = jnp.where(mine, tg, padded * pnz)
    tg_far = jnp.where(mine, padded * pnz, tg)

    smem = pl.BlockSpec(memory_space=pltpu.SMEM)
    hbm = pl.BlockSpec(memory_space=pl.ANY)
    vmem = pl.BlockSpec(memory_space=pltpu.VMEM)
    block = (size, size)
    pool = pltpu.VMEM((padded * nnz + 1,) + block, jnp.bfloat16)
    gram = pltpu.VMEM((padded * pnz + 1,) + block, jnp.bfloat16)
    edge = 2 * BAND * pnz
    out_type = jax.ShapeDtypeStruct((rows * pnz,) + block, jnp.bfloat16)
    product = 2 * size ** 3
    out, part = pl.pallas_call(
        partial(first_kernel, scale),
        out_shape=(out_type, jax.ShapeDtypeStruct((edge,) + block, jnp.float32)),
        in_specs=[smem] * 4 + [hbm] * 3,
        out_specs=(hbm, vmem),
        scratch_shapes=[
            pool,
            gram,
            pltpu.VMEM(((rows - 2 * BAND) * pnz,) + block, jnp.bfloat16),
            pltpu.SemaphoreType.DMA((4,)),
        ],
        compiler_params=pltpu.CompilerParams(vmem_limit_bytes=48 * MIB),
        cost_estimate=pl.CostEstimate(
            flops=rows * 2 * nnz * pnz * product, bytes_accessed=16 * MIB, transcendentals=0
        ),
    )(dx, dp, tx, tg_own, x, low, high)
    out = pl.pallas_call(
        partial(second_kernel, scale),
        out_shape=out_type,
        in_specs=[smem] * 4 + [hbm] * 7,
        out_specs=hbm,
        input_output_aliases={10: 0},
        scratch_shapes=[
            pool,
            gram,
            pltpu.VMEM((edge,) + block, jnp.float32),
            pltpu.VMEM((edge,) + block, jnp.bfloat16),
            pltpu.SemaphoreType.DMA((7 + 2 * BAND,)),
        ],
        compiler_params=pltpu.CompilerParams(vmem_limit_bytes=48 * MIB),
        cost_estimate=pl.CostEstimate(
            flops=2 * BAND * 2 * nnz * pnz * product, bytes_accessed=16 * MIB, transcendentals=0
        ),
    )(dx, dp, tx, tg_far, x, low, high, far_low, far_high, part, out)
    return out.reshape(rows, pnz, size, size)


def solution(mesh):
    return jax.shard_map(
        body,
        mesh=mesh,
        in_specs=(
            P(("groups", "grid", "rep"), None, None, None),
            P("groups", None),
            P("groups", None),
        ),
        out_specs=P(("groups", "grid", "rep"), None, None, None),
        check_vma=False,
    )
```

time: 793 us -> 91.4 us (0.12)
  local copies, waits for them, and re-layouts: 368 us -> 4.1 us
  matrix products: 172 us -> 0 us
  loops' own time: 87.5 us -> 0 us
  other arithmetic: 60.7 us -> 0.57 us
  waiting for transfers between devices: 88.8 us -> 49 us
  Pallas kernels: 0 us -> 29.8 us
    dot_general x80 -> x0, matrix products: 172 us -> none  [the longest x32 101 us: pick_blocks(): jnp.einsum('akzy,akp->apzy', far_blocks, select, preferred_element_type=j...]
    gather x64 -> x0, local copies, waits for them, and re-layouts: 155 us -> none  [the longest x32 137 us: pick_blocks(): far_blocks = jnp.take(source_rows, centre + distance, axis=0)]
    dot_general x48 -> x0, local copies, waits for them, and re-layouts: 134 us -> none  [the longest x32 115 us: pick_blocks(): jnp.einsum('akzy,akp->apzy', far_blocks, select, preferred_element_type=j...]
    another operation x2 -> x0, loops' own time: 87.5 us -> none  [the longest x1 55.7 us: body(): return lax.map(update_block_row, jnp.arange(row_count, dtype=jnp.int32))]
    select_n x80 -> x1, other arithmetic: 49.2 us -> 0.07 us  [body(): tg_own = jnp.where(mine, tg, padded * pnz)]
    ppermute x4, waiting for transfers between devices: 88.8 us -> 49 us  [the longest x1 33.7 us: body(): low = lax.ppermute(x[rows * nnz - near:], AXES, forward)]
    dynamic_slice x48 -> x0, local copies, waits for them, and re-layouts: 35.2 us -> none  [the longest x32 20.1 us: body(): gram_rows = lax.map(partial(gram_block_row, padded, BAND), own_rows)]
    dynamic_update_slice x64 -> x0, local copies, waits for them, and re-layouts: 31.1 us -> none  [body(): gram_rows = lax.map(partial(gram_block_row, padded, BAND), own_rows)]
  transfers between devices with their start and end apart: 4 -> 4, of which waited for: 4 -> 2; matrix products, arithmetic and copies ran while one was open for 0% -> 1% of each run, Pallas kernels for 0% -> 22%
where the time goes in v1:
time: 91.4 us; the launch traced here: 91.1 us
  waiting for transfers between devices  49 us (54%)
  Pallas kernels  29.8 us (33%)
  starting transfers between devices  7.51 us (8%)
  local copies, waits for them, and re-layouts  4.1 us (4%)
    ppermute x1, waiting for transfers between devices, body(): low = lax.ppermute(x[rows * nnz - near:], AXES, forward)  33.7 us
    pallas_call x1, Pallas kernels, body(): pl.pallas_call(partial(first_kernel, scale), out_shape=(out_type, jax.Sha...  20.1 us
    ppermute x1, waiting for transfers between devices, body(): high = lax.ppermute(x[:near], AXES, backward)  15.3 us
    pallas_call x1, Pallas kernels, body(): pl.pallas_call(partial(second_kernel, scale), out_shape=out_type, in_spec...  9.7 us
    ppermute x1, starting transfers between devices, body(): high = lax.ppermute(x[:near], AXES, backward)  5.45 us
    slice x1, local copies, waits for them, and re-layouts, body(): far_high = lax.ppermute(x[near:2 * near], AXES, backward)  3.77 us
    ppermute x1, starting transfers between devices, body(): low = lax.ppermute(x[rows * nnz - near:], AXES, forward)  1.86 us
  transfers between devices with their start and end apart: 4, of which 2 were waited for; matrix products, arithmetic and copies ran while one was open for 1% of the time, Pallas kernels for 22%

profile of v1, /device:TPU:0, one launch (start us, length us, event | category | flops | bytes accessed | tf_op | source)
XLA Modules:
  0.0 91.1 jit_solution(4130049053907653816)
XLA Ops:
  0.0 0.0 copy-start
  0.0 0.0 copy-start.2
  0.0 0.0 copy-start.1
  0.0 3.8 %fusion.8 = (bf16[4,6,128,128]{3,2,1,0:T(8,128)(2,1)}, bf16[4,6,128,128]{3,2,1,0:T(8,128)(2,1)}, bf16[4,6,128,128]{3,2,1,0:T(8,128)(2,1)}, bf16[4,6,128,128]{3,2,1,0:T(8,128)(2,1)}) fusion(bf16[16,6,128,128]{3,2,1,0:T(8,128)(2,1)} %param.3), kind=kLoop, calls=%fused_computation.29 | loop fusion | bytes 6291456 | tf_op jit(solution)/shard_map/slice | solution.py:191
  3.8 5.5 %collective-permute-start.1 = (bf16[24,128,128]{2,1,0:T(8,128)(2,1)}, bf16[24,128,128]{2,1,0:T(8,128)(2,1)}, u32[]{:S(2)}, u32[]{:S(2)}) collective-permute-start(bf16[24,128,128]{2,1,0:T(8,128)(2,1)} %bitcast.2), channel_id=1, source_target_pairs={{1,0},{2,1},{3,2},{4,3},{5,4},{6,5},{7,6},{8,7},{9,8},{10,9},{11,1... | collective-permute-start | bytes 2359304 | tf_op jit(solution)/shard_map/ppermute | solution.py:189
  9.2 0.2 collective-permute-start.3
  9.4 1.9 %collective-permute-start = (bf16[24,128,128]{2,1,0:T(8,128)(2,1)}, bf16[24,128,128]{2,1,0:T(8,128)(2,1)}, u32[]{:S(2)}, u32[]{:S(2)}) collective-permute-start(bf16[24,128,128]{2,1,0:T(8,128)(2,1)} %bitcast.1), channel_id=1, source_target_pairs={{0,1},{1,2},{2,3},{3,4},{4,5},{5,6},{6,7},{7,8},{8,9},{9,10},{10,1... | collective-permute-start | bytes 2359304 | tf_op jit(solution)/shard_map/ppermute | solution.py:188
  11.3 0.0 collective-permute-start.2
  11.3 0.0 copy-done.2
  11.4 0.1 fusion.10
  11.4 0.0 copy-done.1
  11.4 0.1 fusion.7
  11.5 0.1 fusion.9
  11.6 0.1 fusion.5
  11.7 0.1 select_reduce_fusion.1
  11.8 0.2 select_reduce_fusion
  12.0 0.1 add_select_fusion.1
  12.1 0.1 copy.13.dx
  12.1 0.1 copy.14.dp
  12.2 15.3 %collective-permute-done.1.high = bf16[24,128,128]{2,1,0:T(8,128)(2,1)} collective-permute-done((bf16[24,128,128]{2,1,0:T(8,128)(2,1)}, bf16[24,128,128]{2,1,0:T(8,128)(2,1)}, u32[]{:S(2)}, u32[]{:S(2)}) %collective-permute-start.1) | collective-permute-done | bytes 786464 | tf_op jit(solution)/shard_map/ppermute | solution.py:189
  27.5 33.7 %collective-permute-done.low = bf16[24,128,128]{2,1,0:T(8,128)(2,1)} collective-permute-done((bf16[24,128,128]{2,1,0:T(8,128)(2,1)}, bf16[24,128,128]{2,1,0:T(8,128)(2,1)}, u32[]{:S(2)}, u32[]{:S(2)}) %collective-permute-start) | collective-permute-done | bytes 786464 | tf_op jit(solution)/shard_map/ppermute | solution.py:188
  61.2 0.0 copy-done
  61.2 20.1 %shard_map.37 = (bf16[160,128,128]{2,1,0:T(8,128)(2,1)}, f32[80,128,128]{2,1,0:T(8,128)}) custom-call(s32[32,6]{1,0:T(8,128)S(1)} %copy.13.dx, s32[32,10]{1,0:T(8,128)S(1)} %copy.14.dp, s32[32,32]{1,0:T(8,128)S(1)} %get-tuple-element.19.tx, s32[32,32]{1,0:T(8,128)S(1)} %get-tuple-element.13.tg, bf16[96,128,128]{2,1,0:T(8,128)(2,1)S(1)} %bitcast.7, ...), custom_call_target="tpu_custom_call" | custom-call | flops 8053063680 | bytes 16777216 | tf_op jit(solution)/shard_map/pallas_call | solution.py:209
  81.4 0.0 collective-permute-done.3.far_high
  81.4 0.0 collective-permute-done.2.far_low
  81.4 9.7 %shard_map.38 = bf16[160,128,128]{2,1,0:T(8,128)(2,1)} custom-call(s32[32,6]{1,0:T(8,128)S(1)} %copy.13.dx, s32[32,10]{1,0:T(8,128)S(1)} %copy.14.dp, s32[32,32]{1,0:T(8,128)S(1)} %get-tuple-element.19.tx, s32[32,32]{1,0:T(8,128)S(1)} %get-tuple-element.14.tg, bf16[96,128,128]{2,1,0:T(8,128)(2,1)} %bitcast.6, ...), custom_call_target="tpu_custom_call", output_to_operand_aliasing={{}: (10, {})} | custom-call | flops 4026531840 | bytes 16777216 | tf_op jit(solution)/shard_map/pallas_call | solution.py:225
  (6 shorter events, 0.1 us)
Async XLA Ops:
  0.0 61.2 %copy-start = (bf16[16,6,128,128]{3,2,1,0:T(8,128)(2,1)S(1)}, bf16[16,6,128,128]{3,2,1,0:T(8,128)(2,1)}, u32[]{:S(2)}) copy-start(bf16[16,6,128,128]{3,2,1,0:T(8,128)(2,1)} %param.3) | copy-start | bytes 9437188
  0.0 11.3 %copy-start.2 = (s32[256,6]{0,1:T(8,128)S(1)}, s32[256,6]{0,1:T(8,128)}, u32[]{:S(2)}) copy-start(s32[256,6]{0,1:T(8,128)} %param.4) | copy-start | bytes 18436
  0.0 11.4 %copy-start.1 = (s32[256,10]{0,1:T(8,128)S(1)}, s32[256,10]{0,1:T(8,128)}, u32[]{:S(2)}) copy-start(s32[256,10]{0,1:T(8,128)} %param.5) | copy-start | bytes 30724
  3.8 23.7 %collective-permute-start.1 = (bf16[24,128,128]{2,1,0:T(8,128)(2,1)}, bf16[24,128,128]{2,1,0:T(8,128)(2,1)}, u32[]{:S(2)}, u32[]{:S(2)}) collective-permute-start(bf16[24,128,128]{2,1,0:T(8,128)(2,1)} %bitcast.2), channel_id=1, source_target_pairs={{1,0},{2,1},{3,2},{4,3},{5,4},{6,5},{7,6},{8,7},{9,8},{10,9},{11,1... | collective-permute-start | bytes 2359304 | tf_op jit(solution)/shard_map/ppermute | solution.py:189
  9.2 72.1 %collective-permute-start.3 = (bf16[24,128,128]{2,1,0:T(8,128)(2,1)}, bf16[24,128,128]{2,1,0:T(8,128)(2,1)}, u32[]{:S(2)}, u32[]{:S(2)}) collective-permute-start(bf16[24,128,128]{2,1,0:T(8,128)(2,1)} %bitcast.4), channel_id=1, source_target_pairs={{1,0},{2,1},{3,2},{4,3},{5,4},{6,5},{7,6},{8,7},{9,8},{10,9},{11,1... | collective-permute-start | bytes 2359304 | tf_op jit(solution)/shard_map/ppermute | solution.py:191
  9.4 51.8 %collective-permute-start = (bf16[24,128,128]{2,1,0:T(8,128)(2,1)}, bf16[24,128,128]{2,1,0:T(8,128)(2,1)}, u32[]{:S(2)}, u32[]{:S(2)}) collective-permute-start(bf16[24,128,128]{2,1,0:T(8,128)(2,1)} %bitcast.1), channel_id=1, source_target_pairs={{0,1},{1,2},{2,3},{3,4},{4,5},{5,6},{6,7},{7,8},{8,9},{9,10},{10,1... | collective-permute-start | bytes 2359304 | tf_op jit(solution)/shard_map/ppermute | solution.py:188
  11.3 70.1 %collective-permute-start.2 = (bf16[24,128,128]{2,1,0:T(8,128)(2,1)}, bf16[24,128,128]{2,1,0:T(8,128)(2,1)}, u32[]{:S(2)}, u32[]{:S(2)}) collective-permute-start(bf16[24,128,128]{2,1,0:T(8,128)(2,1)} %bitcast.3), channel_id=1, source_target_pairs={{0,1},{1,2},{2,3},{3,4},{4,5},{5,6},{6,7},{7,8},{8,9},{9,10},{10,1... | collective-permute-start | bytes 2359304 | tf_op jit(solution)/shard_map/ppermute | solution.py:190

commit v2 on v0

v2 whole, which is shorter than its diff:
```python
from functools import partial

import jax
import jax.numpy as jnp
from jax import lax
from jax.experimental import pallas as pl
from jax.experimental.pallas import tpu as pltpu
from jax.sharding import PartitionSpec as P

BAND = 4
REACH = 2 * BAND
CENTRE = 3 * BAND
AXES = ("grid", "rep")
MIB = 1024 * 1024
FIRST = 12
STEPS = 8
BIG = 60
TO_X, TO_GRAM, TO_FAR, TO_HALO = 0, 32, 64, 96
LANES = 128
SPARE = 25
SENT = TO_HALO + SPARE


def shift_lane(s):
    return TO_X + SPARE + s


def want_lane(p):
    free = 32 - SPARE
    return (TO_GRAM + SPARE + p) if p < free else (TO_FAR + SPARE + p - free)


def bit_count(v):
    v = v - ((v >> 1) & 0x55555555)
    v = (v & 0x33333333) + ((v >> 2) & 0x33333333)
    v = (v + (v >> 4)) & 0x0F0F0F0F
    return (v + (v >> 8) + (v >> 16)) & 0x3F


def plan_kernel(dims, me, x_cols, p_cols, ints, largest):
    rows, nnz, pnz = dims
    total = x_cols.shape[1]
    padded = rows + 2 * REACH
    most = BAND * nnz
    edge = 2 * BAND * pnz
    lane = lax.broadcasted_iota(jnp.int32, (8, total), 1)
    sub = lax.broadcasted_iota(jnp.int32, (8, total), 0)

    def offsets(ref, count, reach):
        index = lax.broadcasted_iota(jnp.int32, (count, total), 1)
        off = ref[...] - index
        off = jnp.where(off < -reach, off + total, off)
        return jnp.where(off > reach, off - total, off)

    x_off, p_off = offsets(x_cols, nnz, BAND), offsets(p_cols, pnz, REACH)

    def masks(off, reach, axis):
        one = jnp.int32(1)
        parts = [
            lax.slice_in_dim(off, s, s + 1, axis=axis) for s in range(off.shape[axis])
        ]
        return sum(one << (part + reach) for part in parts)

    x_mask = jnp.broadcast_to(masks(x_off, BAND, 0), (8, total))
    p_mask = jnp.broadcast_to(masks(p_off, REACH, 0), (8, total))

    def framed(mask, t, left):
        return pltpu.roll(mask, (REACH - t) % total, 1) << left

    x_frame = [framed(x_mask, t, t) for t in range(2 * REACH)]
    p_frame = {t: framed(p_mask, t, t - BAND) for t in range(BAND, 3 * BAND)}

    def holds(mask, t):
        return -((mask >> (t + BAND)) & 1)

    def side(i, k, far):
        wanted = {}
        for tk in range(k, k + BAND):
            found = jnp.zeros_like(x_mask)
            for ti in range(i, i + BAND):
                found = found | (p_frame[ti] & holds(x_frame[ti], tk))
            wanted[tk] = found & p_frame[tk]
        used = []
        for tf in range(far, far + BAND):
            found = jnp.zeros_like(x_mask)
            for tk in range(k, k + BAND):
                found = found | (wanted[tk] & holds(x_frame[tk], tf))
            used.append((found & x_frame[tf]) >> tf)
        return used

    up, down = side(REACH, BAND, 0), side(BAND, REACH, 3 * BAND)
    needed = jnp.maximum(sum(map(bit_count, up)), sum(map(bit_count, down)))
    needed = jnp.where(lane % rows == 0, needed, 0)
    largest[...] = jnp.broadcast_to(jnp.max(needed, axis=(0, 1), keepdims=True), largest.shape)

    used = jnp.zeros_like(x_mask)
    for q, mask in enumerate(up + down):
        used = jnp.where(sub == q, mask, used)
    here = me[0] * rows
    above = jnp.where(here + rows == total, 0, here + rows)
    at_here = jnp.sum(jnp.where(lane == here, used, 0), axis=1, keepdims=True)
    at_above = jnp.sum(jnp.where(lane == above, used, 0), axis=1, keepdims=True)

    def one(column, q):
        return lax.slice_in_dim(column, q, q + 1, axis=0)

    row = lax.broadcasted_iota(jnp.int32, (padded, 1), 0)
    wide_lane = lax.broadcasted_iota(jnp.int32, (padded, total), 1)
    wide_row = lax.broadcasted_iota(jnp.int32, (padded, total), 0)
    source = here - REACH + wide_row
    source = jnp.where(source < 0, source + total, source)
    source = jnp.where(source >= total, source - total, source)
    pick = (wide_lane == source).astype(jnp.float32)

    def picked(off):
        return lax.dot_general(
            pick, off.astype(jnp.float32), (((1,), (1,)), ((), ())),
            preferred_element_type=jnp.float32,
        ).astype(jnp.int32)

    dx, dp = picked(x_off), picked(p_off)
    x_row, p_row = masks(dx, BAND, 1), masks(dp, REACH, 1)
    far_row = jnp.zeros((padded, 1), jnp.int32)
    far_base = jnp.zeros((padded, 1), jnp.int32)
    sent = jnp.zeros((padded, 1), jnp.int32)
    base_low = jnp.zeros((1, 1), jnp.int32)
    base_high = jnp.full((1, 1), most, jnp.int32)
    for q in range(BAND):
        t = BAND - 1 - q
        low, high = one(at_here, t), one(at_above, BAND + q)
        place = padded - BAND + q
        far_row = jnp.where(row == t, low, jnp.where(row == place, high, far_row))
        far_base = jnp.where(row == t, base_low, jnp.where(row == place, base_high, far_base))
        base_low = base_low + bit_count(low)
        base_high = base_high + bit_count(high)
        sent = jnp.where(row == rows + t, one(at_above, t), sent)
        sent = jnp.where(row == REACH + BAND + q, one(at_here, BAND + q), sent)

    column = lax.broadcasted_iota(jnp.int32, (padded, LANES), 1)
    place = column & 31

    def looked_up(mask, reach):
        at = place - (CENTRE - reach)
        inside = (at >= 0) & (at <= 2 * reach)
        at = jnp.where(inside, at, 0)
        return inside & (((mask >> at) & 1) == 1), bit_count(mask & ((1 << at) - 1))

    close = (row >= BAND) & (row < padded - BAND)
    own = (row >= REACH) & (row < REACH + rows)
    x_hit, x_slot = looked_up(x_row, BAND)
    p_hit, p_slot = looked_up(p_row, REACH)
    far_hit, far_rank = looked_up(far_row, BAND)
    halo = jnp.where(row < REACH, row - BAND, row - rows - REACH + BAND) * pnz
    table = jnp.where(x_hit & close, row * nnz + x_slot, padded * nnz)
    to_gram = jnp.where(p_hit & own, (row - REACH) * pnz + p_slot, rows * pnz)
    to_far = jnp.where(far_hit, far_base + far_rank, 2 * most)
    to_halo = jnp.where(p_hit & close & ~own, halo + p_slot, edge)
    table = jnp.where(column >= TO_GRAM, to_gram, table)
    table = jnp.where(column >= TO_FAR, to_far, table)
    table = jnp.where(column >= TO_HALO, to_halo, table)
    for s in range(nnz):
        table = jnp.where(column == shift_lane(s), lax.slice_in_dim(dx, s, s + 1, axis=1), table)
    for p in range(pnz):
        table = jnp.where(column == want_lane(p), lax.slice_in_dim(dp, p, p + 1, axis=1), table)
    ints[...] = jnp.where(column == SENT, sent, table)


def products(dims, ints, r, slots, table, left, right, base=0):
    _, nnz, pnz = dims
    shift = {s: ints[r, shift_lane(s)] for s in slots}
    want = [ints[r, want_lane(p)] + CENTRE for p in range(pnz)]
    own = jnp.concatenate([left[r * nnz + s - base] for s in slots], axis=1)
    size = left.shape[1]
    blocks = []
    for p in range(0, pnz, 2):
        columns = [
            jnp.concatenate(
                [right[ints[r + shift[s], table + want[q] - shift[s]]] for s in slots], axis=0
            )
            for q in (p, p + 1)
        ]
        pair = jnp.dot(
            own, jnp.concatenate(columns, axis=1), preferred_element_type=jnp.float32
        )
        blocks += [pair[:, :size], pair[:, size:]]
    return blocks


def clear(ref):
    ref[ref.shape[0] - 1] = jnp.zeros(ref.shape[1:], ref.dtype)


def begin(sems, moves):
    copies = []
    for n, (source, target, place) in enumerate(moves):
        copy = pltpu.make_async_copy(
            source, target.at[pl.ds(place, source.shape[0])], sems.at[n]
        )
        copy.start()
        copies.append(copy)
    return copies


def finish(copies):
    for copy in copies:
        copy.wait()


def gather(dims, ints, pool, outs, picks, sem):
    rows, nnz, _ = dims
    copies = []
    for side, arrays in enumerate(outs):
        for n in range(BAND * nnz):
            picks[side, n] = REACH * nnz
        count = jnp.int32(0)
        for q in range(BAND):
            r = REACH + rows - BAND - 1 - q if side == 0 else REACH + BAND + q
            for s in range(nnz):
                picks[side, count] = r * nnz + s
                count = count + ((ints[r, SENT] >> (ints[r, shift_lane(s)] + BAND)) & 1)
        n = 0
        for out in arrays:
            for place in range(out.shape[0]):
                copy = pltpu.make_async_copy(
                    pool.at[pl.ds(picks[side, n], 1)], out.at[pl.ds(place, 1)], sem.at[side, n]
                )
                copy.start()
                copies.append(copy)
                n += 1
    return copies


def inner_kernel(
    dims, scale, ints, x, out, up, down, up_rest, down_rest, pool, gram, picks, sems, pick_sems
):
    rows, nnz, pnz = dims
    copies = begin(sems, [(x, pool, REACH * nnz)])
    clear(pool)
    finish(copies)
    outs = ((up, up_rest), (down, down_rest))
    listed = gather(dims, ints, pool, outs, picks, pick_sems)

    @pl.loop(0, rows - 2 * BAND)
    def _(i):
        r = REACH + BAND + i
        for p, block in enumerate(products(dims, ints, r, range(nnz), TO_X, pool, pool)):
            gram[i * pnz + p] = (block * scale).astype(gram.dtype)

    finish(begin(sems, [(gram, out, 0)]) + listed)


def near_kernel(
    dims, scale, ints, x, low, high, inner, out, part, gram_part, pool, gram, done, kept_sums,
    near_sums, sems
):
    rows, nnz, pnz = dims
    start = REACH * nnz
    edge = BAND * pnz
    own, near = x.shape[0], low.shape[0]
    half = own // 2
    copies = begin(sems, [
        (low, pool, start - near), (x.at[pl.ds(0, half)], pool, start),
        (high, pool, start + own), (x.at[pl.ds(half, half)], pool, start + half),
        (inner, gram, edge),
    ])
    clear(pool)
    clear(gram)

    def edge_grams(first_row, halo_row, place):
        @pl.loop(0, BAND)
        def _(e):
            i = first_row + e
            blocks = products(dims, ints, REACH + i, range(nnz), TO_X, pool, pool)
            for p, block in enumerate(blocks):
                gram[i * pnz + p] = (block * scale).astype(gram.dtype)

        @pl.loop(0, BAND)
        def _(e):
            r = REACH + halo_row + e
            blocks = products(dims, ints, r, range(nnz), TO_X, pool, pool)
            for p, block in enumerate(blocks):
                near_sums[(place + e) * pnz + p] = block

    finish(copies[:2])
    edge_grams(0, -BAND, 0)
    finish(copies[2:4])
    edge_grams(rows - BAND, rows, BAND)
    finish(copies[4:])
    first = begin(sems.at[pl.ds(0, 1)], [(near_sums, gram_part, 0)])

    def update(r, store):
        blocks = products(dims, ints, r, range(nnz), TO_GRAM, pool, gram)
        for p, block in enumerate(blocks):
            kept = pool[ints[r, TO_X + ints[r, want_lane(p)] + CENTRE]].astype(jnp.float32)
            store(p, 1.5 * kept - 0.5 * block)

    @pl.loop(0, 2 * BAND)
    def _(e):
        def store(p, value):
            kept_sums[e * pnz + p] = value

        update(REACH + jnp.where(e < BAND, e, rows - 2 * BAND + e), store)

    second = begin(sems.at[pl.ds(1, 1)], [(kept_sums, part, 0)])

    @pl.loop(BAND, rows - BAND)
    def _(i):
        def store(p, value):
            done[(i - BAND) * pnz + p] = value.astype(done.dtype)

        update(REACH + i, store)

    third = begin(sems.at[pl.ds(2, 1)], [(done, out, edge)])
    finish(first + second + third)


def far_kernel(
    dims, scale, ints, x, low, high, far_low, far_high, more, part, gram_part, unused, out, pool, far, gram, near_sums, kept_sums, done, sems
):
    rows, nnz, pnz = dims
    near = low.shape[0]
    own = x.shape[0]
    start = BAND * nnz
    edge = BAND * pnz
    first = far_low.shape[0]
    extra = more.shape[0] // 2
    moves = [
        (more.at[pl.ds(0, extra)], far, first),
        (more.at[pl.ds(extra, extra)], far, 2 * first + extra),
        (far_low, far, 0),
        (far_high, far, first + extra),
        (low, pool, start - near),
        (high, pool, start + own),
        (x.at[pl.ds(0, near)], pool, start),
        (x.at[pl.ds(own - near, near)], pool, start + own - near),
    ]
    copies = begin(sems, moves)
    used = len(moves) + 4
    late = begin(sems.at[pl.ds(len(moves), 4)], [
        (half.at[pl.ds(e, edge)], target, e)
        for half, target in ((gram_part, near_sums), (part, kept_sums))
        for e in (0, edge)
    ])
    clear(far)
    clear(gram)
    finish(copies)
    offset = (REACH - BAND) * nnz

    for e in range(2 * BAND):
        if e % BAND == 0:
            late[e // BAND].wait()
        if e < BAND:
            r, slots = REACH - BAND + e, range(0, BAND - e)
        else:
            r, slots = REACH + rows - BAND + e, range(nnz - 1 - (e - BAND), nnz)
        blocks = products(dims, ints, r, slots, TO_FAR, pool, far, offset)
        for p, block in enumerate(blocks):
            n = e * pnz + p
            gram[n] = ((near_sums[n] + block) * scale).astype(gram.dtype)

    outgoing = []
    for e in range(2 * BAND):
        if e % BAND == 0:
            late[2 + e // BAND].wait()
        if e < BAND:
            i, slots = e, range(0, BAND - e)
        else:
            i, slots = rows - 2 * BAND + e, range(nnz - 1 - (e - BAND), nnz)
        blocks = products(dims, ints, REACH + i, slots, TO_HALO, pool, gram, offset)
        for p, block in enumerate(blocks):
            n = e * pnz + p
            done[n] = (kept_sums[n] - 0.5 * block).astype(done.dtype)
        outgoing += begin(
            sems.at[pl.ds(used + e, 1)], [(done.at[pl.ds(e * pnz, pnz)], out, i * pnz)]
        )
    finish(outgoing)


def body(x_vals, x_cols, p_cols):
    rows, nnz, size, _ = x_vals.shape
    pnz = p_cols.shape[1]
    count = lax.axis_size(AXES)
    me = lax.axis_index(AXES)
    first_row = me * rows
    scale = 1.0 / (4 * nnz * size)
    padded = rows + 2 * REACH
    forward = [(i, (i + 1) % count) for i in range(count)]
    backward = [(target, source) for source, target in forward]
    near = BAND * nnz
    edge = 2 * BAND * pnz
    most = near
    first = min(FIRST, most)
    product = 2 * size ** 3
    block = (size, size)

    smem = pl.BlockSpec(memory_space=pltpu.SMEM)
    hbm = pl.BlockSpec(memory_space=pl.ANY)
    vmem = pl.BlockSpec(memory_space=pltpu.VMEM)

    def shaped(blocks, kind=jnp.bfloat16):
        return jax.ShapeDtypeStruct((blocks,) + block, kind)

    def scratch(blocks, kind=jnp.bfloat16):
        return pltpu.VMEM((blocks,) + block, kind)

    def settings(mib):
        return pltpu.CompilerParams(vmem_limit_bytes=mib * MIB)

    def cost(products_made, blocks_moved):
        return pl.CostEstimate(
            flops=products_made * product, bytes_accessed=blocks_moved * 2 * size * size,
            transcendentals=0,
        )

    x = x_vals.reshape(rows * nnz, size, size)
    low = lax.ppermute(x[rows * nnz - near:], AXES, forward)
    high = lax.ppermute(x[:near], AXES, backward)

    dims = (rows, nnz, pnz)
    ints, largest = pl.pallas_call(
        partial(plan_kernel, dims),
        out_shape=(
            jax.ShapeDtypeStruct((padded, LANES), jnp.int32),
            jax.ShapeDtypeStruct((8, LANES), jnp.int32),
        ),
        in_specs=[smem, vmem, vmem],
        out_specs=(vmem, vmem),
        compiler_params=settings(BIG),
    )(me.astype(jnp.int32).reshape(1), x_cols.T, p_cols.T)
    largest = lax.pmax(largest[0, 0], "groups")

    lists = pltpu.SMEM((2, 32), jnp.int32)
    remaining = most - first
    inner, up, down, up_rest, down_rest = pl.pallas_call(
        partial(inner_kernel, dims, scale),
        out_shape=[
            shaped((rows - 2 * BAND) * pnz), shaped(first), shaped(first), shaped(remaining),
            shaped(remaining),
        ],
        in_specs=[smem, hbm],
        out_specs=[hbm] * 5,
        scratch_shapes=[
            scratch(padded * nnz + 1),
            scratch((rows - 2 * BAND) * pnz),
            lists,
            pltpu.SemaphoreType.DMA((1,)),
            pltpu.SemaphoreType.DMA((2, most)),
        ],
        compiler_params=settings(BIG),
        cost_estimate=cost((rows - 2 * BAND) * nnz * pnz, 200),
    )(ints, x)
    far_low = lax.ppermute(up, AXES, forward)
    far_high = lax.ppermute(down, AXES, backward)

    def near_step(low, high, inner):
        return pl.pallas_call(
            partial(near_kernel, dims, scale),
            out_shape=[
                shaped(rows * pnz), shaped(edge, jnp.float32), shaped(edge, jnp.float32)
            ],
            in_specs=[smem] + [hbm] * 4,
            out_specs=[hbm] * 3,
            scratch_shapes=[
                scratch(padded * nnz + 1),
                scratch(rows * pnz + 1),
                scratch((rows - 2 * BAND) * pnz),
                scratch(edge, jnp.float32),
                scratch(edge, jnp.float32),
                pltpu.SemaphoreType.DMA((5,)),
            ],
            compiler_params=settings(BIG),
            cost_estimate=cost((4 * BAND + rows) * nnz * pnz, 900),
        )(ints, x, low, high, inner)

    def step(many, up, down, low, high, inner):
        blank = jnp.zeros((remaining - many,) + block, jnp.bfloat16)
        more = [blank, blank]
        if many:
            more_low = lax.ppermute(up[:many], AXES, forward)
            more_high = lax.ppermute(down[:many], AXES, backward)
            more = [more_low, blank, more_high, blank]
        return *near_step(low, high, inner), jnp.concatenate(more)

    sizes = [n for n in range(remaining) if n <= STEPS] + [remaining]
    out, part, gram_part, more = lax.switch(
        sum((largest > first + n).astype(jnp.int32) for n in sizes[:-1]),
        [partial(step, many) for many in sizes], up_rest, down_rest, low, high, inner,
    )

    operands = [
        ints, x, low, high, far_low, far_high, more, part, gram_part, out
    ]
    out = pl.pallas_call(
        partial(far_kernel, dims, scale),
        out_shape=shaped(rows * pnz),
        in_specs=[smem] + [hbm] * (len(operands) - 1),
        out_specs=hbm,
        input_output_aliases={len(operands) - 1: 0},
        scratch_shapes=[
            scratch((rows + 2 * BAND) * nnz),
            scratch(2 * most + 1),
            scratch(edge + 1),
            scratch(edge, jnp.float32),
            scratch(edge, jnp.float32),
            scratch(edge),
            pltpu.SemaphoreType.DMA((12 + 2 * BAND,)),
        ],
        compiler_params=settings(BIG),
        cost_estimate=cost(2 * BAND * nnz * pnz, 600),
    )(*operands)
    return out.reshape(rows, pnz, size, size)


def solution(mesh):
    return jax.shard_map(
        body,
        mesh=mesh,
        in_specs=(
            P(("groups", "grid", "rep"), None, None, None),
            P("groups", None),
            P("groups", None),
        ),
        out_specs=P(("groups", "grid", "rep"), None, None, None),
        check_vma=False,
    )
```

time: 793 us -> 81 us (0.10)
  local copies, waits for them, and re-layouts: 368 us -> 5.08 us
  matrix products: 172 us -> 0 us
  loops' own time: 87.5 us -> 0.04 us
  waiting for transfers between devices: 88.8 us -> 8.26 us
  other arithmetic: 60.7 us -> 1 us
  Pallas kernels: 0 us -> 36.9 us
  starting transfers between devices: 9.95 us -> 18.1 us
    dot_general x80 -> x0, matrix products: 172 us -> none  [the longest x32 101 us: pick_blocks(): jnp.einsum('akzy,akp->apzy', far_blocks, select, preferred_element_type=j...]
    gather x64 -> x0, local copies, waits for them, and re-layouts: 155 us -> none  [the longest x32 137 us: pick_blocks(): far_blocks = jnp.take(source_rows, centre + distance, axis=0)]
    dot_general x48 -> x0, local copies, waits for them, and re-layouts: 134 us -> none  [the longest x32 115 us: pick_blocks(): jnp.einsum('akzy,akp->apzy', far_blocks, select, preferred_element_type=j...]
    another operation x2 -> x1, loops' own time: 87.5 us -> 0.04 us  [body(): lax.switch(sum(((largest > first + n).astype(jnp.int32) for n in sizes[:-...]
    ppermute x4 -> x6, waiting for transfers between devices: 88.8 us -> 8.26 us  [the longest x1 8.25 us: body(): high = lax.ppermute(x[:near], AXES, backward)]
    select_n x80 -> x0, other arithmetic: 49.2 us -> none  [the longest x48 48.7 us: pick_blocks(): far_blocks = jnp.take(source_rows, centre + distance, axis=0)]
    pallas_call x0 -> x4, Pallas kernels: none -> 36.9 us  [the longest x1 18.2 us: near_step(): pl.pallas_call(partial(near_kernel, dims, scale), out_shape=[shaped(rows...]
    dynamic_slice x48 -> x0, local copies, waits for them, and re-layouts: 35.2 us -> none  [the longest x32 20.1 us: body(): gram_rows = lax.map(partial(gram_block_row, padded, BAND), own_rows)]
  transfers between devices with their start and end apart: 4 -> 6, of which waited for: 4 -> 1; matrix products, arithmetic and copies ran while one was open for 0% -> 4% of each run, Pallas kernels for 0% -> 37%
where the time goes in v2:
time: 81 us; the launch traced here: 80.2 us
  Pallas kernels  36.9 us (46%)
  starting transfers between devices  18.1 us (22%)
  waiting for transfers between devices  8.26 us (10%)
  between operations  5.97 us (7%)
  local copies, waits for them, and re-layouts  5.08 us (6%)
  blocking collectives  4.91 us (6%)
  other arithmetic  1 us (1%)
    pallas_call x1, Pallas kernels, near_step(): pl.pallas_call(partial(near_kernel, dims, scale), out_shape=[shaped(rows...  18.2 us
    pallas_call x1, Pallas kernels, body(): pl.pallas_call(partial(inner_kernel, dims, scale), out_shape=[shaped((row...  9.26 us
    ppermute x1, waiting for transfers between devices, body(): high = lax.ppermute(x[:near], AXES, backward)  8.25 us
    pallas_call x1, Pallas kernels, body(): pl.pallas_call(partial(far_kernel, dims, scale), out_shape=shaped(rows *...  7.57 us
    ppermute x1, starting transfers between devices, step(): more_low = lax.ppermute(up[:many], AXES, forward)  6.5 us
    pmax x1, blocking collectives, body(): largest = lax.pmax(largest[0, 0], 'groups')  4.91 us
    ppermute x1, starting transfers between devices, body(): far_high = lax.ppermute(down, AXES, backward)  4.43 us
    ppermute x1, starting transfers between devices, body(): low = lax.ppermute(x[rows * nnz - near:], AXES, forward)  3.02 us
  transfers between devices with their start and end apart: 6, of which 1 were waited for; matrix products, arithmetic and copies ran while one was open for 4% of the time, Pallas kernels for 37%

profile of v2, /device:TPU:0, one launch (start us, length us, event | category | flops | bytes accessed | tf_op | source)
XLA Modules:
  0.0 80.2 jit_solution(16732702237486745504)
XLA Ops:
  0.0 0.0 copy-start
  0.0 2.9 %fusion = (bf16[4,6,128,128]{3,2,1,0:T(8,128)(2,1)}, bf16[4,6,128,128]{3,2,1,0:T(8,128)(2,1)}) fusion(bf16[16,6,128,128]{3,2,1,0:T(8,128)(2,1)} %param.13), kind=kLoop, calls=%fused_computation.9 | loop fusion | bytes 3145728 | tf_op jit(solution)/shard_map/slice | solution.py:417
  2.9 3.0 %collective-permute-start.18 = (bf16[24,128,128]{2,1,0:T(8,128)(2,1)}, bf16[24,128,128]{2,1,0:T(8,128)(2,1)}, u32[]{:S(2)}, u32[]{:S(2)}) collective-permute-start(bf16[24,128,128]{2,1,0:T(8,128)(2,1)} %bitcast.4), channel_id=1, source_target_pairs={{0,1},{1,2},{2,3},{3,4},{4,5},{5,6},{6,7},{7,8},{8,9},{9,10},{10,1... | collective-permute-start | bytes 2359304 | tf_op jit(solution)/shard_map/ppermute | solution.py:416
  5.9 2.4 %collective-permute-start.19 = (bf16[24,128,128]{2,1,0:T(8,128)(2,1)}, bf16[24,128,128]{2,1,0:T(8,128)(2,1)}, u32[]{:S(2)}, u32[]{:S(2)}) collective-permute-start(bf16[24,128,128]{2,1,0:T(8,128)(2,1)} %bitcast.5), channel_id=1, source_target_pairs={{1,0},{2,1},{3,2},{4,3},{5,4},{6,5},{7,6},{8,7},{9,8},{10,9},{11,1... | collective-permute-start | bytes 2359304 | tf_op jit(solution)/shard_map/ppermute | solution.py:417
  8.3 1.9 %shard_map.37 = (s32[32,128]{1,0:T(8,128)}, s32[8,128]{1,0:T(8,128)}) custom-call(s32[1]{0:T(128)} %bitcast.me, s32[6,256]{1,0:T(8,128)} %bitcast.21, s32[10,256]{1,0:T(8,128)} %bitcast.20), custom_call_target="tpu_custom_call" | custom-call | tf_op jit(solution)/shard_map/pallas_call | solution.py:420
  10.2 9.3 %shard_map.38 = (bf16[80,128,128]{2,1,0:T(8,128)(2,1)}, bf16[12,128,128]{2,1,0:T(8,128)(2,1)}, bf16[12,128,128]{2,1,0:T(8,128)(2,1)}, bf16[12,128,128]{2,1,0:T(8,128)(2,1)S(1)}, bf16[12,128,128]{2,1,0:T(8,128)(2,1)}) custom-call(s32[32,128]{1,0:T(8,128)} %get-tuple-element.250.ints, bf16[96,128,128]{2,1,0:T(8,128)(2,1)} %bitcast.8), custom_call_target="tpu_custom_call" | custom-call | flops 2013265920 | bytes 6553600 | tf_op jit(solution)/shard_map/pallas_call | solution.py:434
  19.4 0.1 collective-permute-start.20
  19.5 4.4 %collective-permute-start.21 = (bf16[12,128,128]{2,1,0:T(8,128)(2,1)}, bf16[12,128,128]{2,1,0:T(8,128)(2,1)}, u32[]{:S(2)}, u32[]{:S(2)}) collective-permute-start(bf16[12,128,128]{2,1,0:T(8,128)(2,1)} %get-tuple-element.252), channel_id=1, source_target_pairs={{1,0},{2,1},{3,2},{4,3},{5,4},{6,5},{7,6},{8,7},{9,8},{10,9},{11,1... | collective-permute-start | bytes 1179656 | tf_op jit(solution)/shard_map/ppermute | solution.py:453
  23.9 1.2 %slice.67 = s32[1,1]{1,0:T(1,128)} slice(s32[8,128]{1,0:T(8,128)} %get-tuple-element.253), slice={[0:1], [0:1]} | slice | bytes 8 | tf_op jit(solution)/shard_map/slice | solution.py:430
  25.2 4.9 %pmax.7 = s32[]{:T(128)} all-reduce(s32[]{:T(128)} %bitcast.6), channel_id=1, replica_groups=mesh['groups'=2,'grid'=4,'rep'=4] {'groups'}, use_global_device_ids=true, to_apply=%region_0.0 | all-reduce | flops 1 | bytes 8 | tf_op jit(solution)/shard_map/pmax | solution.py:430
  35.8 0.0 collective-permute-done.18.low
  35.8 8.2 %collective-permute-done.19.high = bf16[24,128,128]{2,1,0:T(8,128)(2,1)} collective-permute-done((bf16[24,128,128]{2,1,0:T(8,128)(2,1)}, bf16[24,128,128]{2,1,0:T(8,128)(2,1)}, u32[]{:S(2)}, u32[]{:S(2)}) %collective-permute-start.19) | collective-permute-done | bytes 786464 | tf_op jit(solution)/shard_map/ppermute | solution.py:417
  44.1 0.0 copy-done
  44.1 28.4 %conditional.1 = (bf16[160,128,128]{2,1,0:T(8,128)(2,1)}, f32[80,128,128]{2,1,0:T(8,128)}, f32[80,128,128]{2,1,0:T(8,128)}, bf16[24,128,128]{2,1,0:T(8,128)(2,1)}) conditional(s32[]{:T(128)} %clamp.3, (s32[32,128]{1,0:T(8,128)}, bf16[96,128,128]{2,1,0:T(8,128)(2,1)S(1)}, bf16[24,128,128]{2,1,0:T(8,128)(2,1)}, ...), branch_computations={%region_1.0_spmd, %region_2.0_spmd, %region_3.0_spmd, %region_4.0_... | conditional | flops 8054243328 | bytes 34209904 | solution.py:485
  44.1 0.9 %slice.51 = bf16[5,128,128]{2,1,0:T(8,128)(2,1)S(1)} slice(bf16[12,128,128]{2,1,0:T(8,128)(2,1)} %get-tuple-element.198), slice={[0:5], [0:128], [0:128]} | slice | bytes 327680 | tf_op jit(solution)/shard_map/cond/branch_5_fun/slice | solution.py:480
  45.0 1.7 %collective-permute-start.9 = (bf16[5,128,128]{2,1,0:T(8,128)(2,1)S(1)}, bf16[5,128,128]{2,1,0:T(8,128)(2,1)S(1)}, u32[]{:S(2)}, u32[]{:S(2)}) collective-permute-start(bf16[5,128,128]{2,1,0:T(8,128)(2,1)S(1)} %slice.51), channel_id=1, source_target_pairs={{1,0},{2,1},{3,2},{4,3},{5,4},{6,5},{7,6},{8,7},{9,8},{10,9},{11,1... | collective-permute-start | bytes 491528 | tf_op jit(solution)/shard_map/cond/branch_5_fun/ppermute | solution.py:480
  46.7 6.5 %collective-permute-start.8 = (bf16[5,128,128]{2,1,0:T(8,128)(2,1)S(1)}, bf16[5,128,128]{2,1,0:T(8,128)(2,1)S(1)}, u32[]{:S(2)}, u32[]{:S(2)}) collective-permute-start(bf16[5,128,128]{2,1,0:T(8,128)(2,1)S(1)} %slice.50), channel_id=1, source_target_pairs={{0,1},{1,2},{2,3},{3,4},{4,5},{5,6},{6,7},{7,8},{8,9},{9,10},{10,1... | collective-permute-start | bytes 491528 | tf_op jit(solution)/shard_map/cond/branch_5_fun/ppermute | solution.py:479
  53.2 18.2 %branch_5_fun.1 = (bf16[160,128,128]{2,1,0:T(8,128)(2,1)}, f32[80,128,128]{2,1,0:T(8,128)}, f32[80,128,128]{2,1,0:T(8,128)}) custom-call(s32[32,128]{1,0:T(8,128)} %get-tuple-element.189.ints, bf16[96,128,128]{2,1,0:T(8,128)(2,1)S(1)} %get-tuple-element.190.x, bf16[24,128,128]{2,1,0:T(8,128)(2,1)} %get-tuple-element.191.low, ...), custom_call_target="tpu_custom_call" | custom-call | flops 8053063680 | bytes 29491200 | tf_op jit(solution)/shard_map/cond/branch_5_fun/pallas_call | solution.py:456
  71.3 0.0 collective-permute-done.9
  71.4 0.0 collective-permute-done.8
  71.4 1.0 %pad_maximum_fusion.4 = bf16[24,128,128]{2,1,0:T(8,128)(2,1)} fusion(bf16[7,128,128]{2,1,0:T(8,128)(2,1)S(1)} %broadcast.23, bf16[5,128,128]{2,1,0:T(8,128)(2,1)S(1)} %collective-permute-done.9, bf16[5,128,128]{2,1,0:T(8,128)(2,1)S(1)} %collective-permute-done.8), kind=kLoop, calls=%fused_computation.4 | loop fusion | flops 1179648 | bytes 1343488 | tf_op jit(solution)/shard_map/cond/branch_5_fun/concatenate | solution.py:482
  72.4 0.0 collective-permute-done.20.far_low
  72.4 0.0 collective-permute-done.21.far_high
  72.4 7.6 %shard_map.39 = bf16[160,128,128]{2,1,0:T(8,128)(2,1)} custom-call(s32[32,128]{1,0:T(8,128)} %get-tuple-element.250.ints, bf16[96,128,128]{2,1,0:T(8,128)(2,1)S(1)} %bitcast.19, bf16[24,128,128]{2,1,0:T(8,128)(2,1)} %collective-permute-done.18.low, bf16[24,128,128]{2,1,0:T(8,128)(2,1)} %collective-permute-done.19.high, ...), custom_call_target="tpu_custom_call", output_to_operand_aliasing={{}: (9, {})} | custom-call | flops 2013265920 | bytes 19660800 | tf_op jit(solution)/shard_map/pallas_call | solution.py:493
  (2 shorter events, 0.0 us)
Async XLA Ops:
  0.0 44.1 %copy-start = (bf16[16,6,128,128]{3,2,1,0:T(8,128)(2,1)S(1)}, bf16[16,6,128,128]{3,2,1,0:T(8,128)(2,1)}, u32[]{:S(2)}) copy-start(bf16[16,6,128,128]{3,2,1,0:T(8,128)(2,1)} %param.13) | copy-start | bytes 9437188
  2.9 32.9 %collective-permute-start.18 = (bf16[24,128,128]{2,1,0:T(8,128)(2,1)}, bf16[24,128,128]{2,1,0:T(8,128)(2,1)}, u32[]{:S(2)}, u32[]{:S(2)}) collective-permute-start(bf16[24,128,128]{2,1,0:T(8,128)(2,1)} %bitcast.4), channel_id=1, source_target_pairs={{0,1},{1,2},{2,3},{3,4},{4,5},{5,6},{6,7},{7,8},{8,9},{9,10},{10,1... | collective-permute-start | bytes 2359304 | tf_op jit(solution)/shard_map/ppermute | solution.py:416
  5.9 38.2 %collective-permute-start.19 = (bf16[24,128,128]{2,1,0:T(8,128)(2,1)}, bf16[24,128,128]{2,1,0:T(8,128)(2,1)}, u32[]{:S(2)}, u32[]{:S(2)}) collective-permute-start(bf16[24,128,128]{2,1,0:T(8,128)(2,1)} %bitcast.5), channel_id=1, source_target_pairs={{1,0},{2,1},{3,2},{4,3},{5,4},{6,5},{7,6},{8,7},{9,8},{10,9},{11,1... | collective-permute-start | bytes 2359304 | tf_op jit(solution)/shard_map/ppermute | solution.py:417
  19.4 53.0 %collective-permute-start.20 = (bf16[12,128,128]{2,1,0:T(8,128)(2,1)}, bf16[12,128,128]{2,1,0:T(8,128)(2,1)}, u32[]{:S(2)}, u32[]{:S(2)}) collective-permute-start(bf16[12,128,128]{2,1,0:T(8,128)(2,1)} %get-tuple-element.251), channel_id=1, source_target_pairs={{0,1},{1,2},{2,3},{3,4},{4,5},{5,6},{6,7},{7,8},{8,9},{9,10},{10,1... | collective-permute-start | bytes 1179656 | tf_op jit(solution)/shard_map/ppermute | solution.py:452
  19.5 52.9 %collective-permute-start.21 = (bf16[12,128,128]{2,1,0:T(8,128)(2,1)}, bf16[12,128,128]{2,1,0:T(8,128)(2,1)}, u32[]{:S(2)}, u32[]{:S(2)}) collective-permute-start(bf16[12,128,128]{2,1,0:T(8,128)(2,1)} %get-tuple-element.252), channel_id=1, source_target_pairs={{1,0},{2,1},{3,2},{4,3},{5,4},{6,5},{7,6},{8,7},{9,8},{10,9},{11,1... | collective-permute-start | bytes 1179656 | tf_op jit(solution)/shard_map/ppermute | solution.py:453
  45.0 26.4 %collective-permute-start.9 = (bf16[5,128,128]{2,1,0:T(8,128)(2,1)S(1)}, bf16[5,128,128]{2,1,0:T(8,128)(2,1)S(1)}, u32[]{:S(2)}, u32[]{:S(2)}) collective-permute-start(bf16[5,128,128]{2,1,0:T(8,128)(2,1)S(1)} %slice.51), channel_id=1, source_target_pairs={{1,0},{2,1},{3,2},{4,3},{5,4},{6,5},{7,6},{8,7},{9,8},{10,9},{11,1... | collective-permute-start | bytes 491528 | tf_op jit(solution)/shard_map/cond/branch_5_fun/ppermute | solution.py:480
  46.7 24.7 %collective-permute-start.8 = (bf16[5,128,128]{2,1,0:T(8,128)(2,1)S(1)}, bf16[5,128,128]{2,1,0:T(8,128)(2,1)S(1)}, u32[]{:S(2)}, u32[]{:S(2)}) collective-permute-start(bf16[5,128,128]{2,1,0:T(8,128)(2,1)S(1)} %slice.50), channel_id=1, source_target_pairs={{0,1},{1,2},{2,3},{3,4},{4,5},{5,6},{6,7},{7,8},{8,9},{9,10},{10,1... | collective-permute-start | bytes 491528 | tf_op jit(solution)/shard_map/cond/branch_5_fun/ppermute | solution.py:479

commit v3 on v2

--- a/solution.py
+++ b/solution.py
@@ -12,8 +12,7 @@
 CENTRE = 3 * BAND
 AXES = ("grid", "rep")
 MIB = 1024 * 1024
-FIRST = 12
-STEPS = 8
+FIRST = 16
 BIG = 60
 TO_X, TO_GRAM, TO_FAR, TO_HALO = 0, 32, 64, 96
 LANES = 128
@@ -206,173 +205,176 @@
         copy.wait()
 
 
-def gather(dims, ints, pool, outs, picks, sem):
+def gather(dims, ints, side, skip, pool, out, picks, sem):
     rows, nnz, _ = dims
+    top = REACH + rows - BAND - 1
+    rows_sent = [top - q if side == 0 else REACH + BAND + q for q in range(BAND)]
+    for n in range(skip + out.shape[0]):
+        picks[n] = rows_sent[0] * nnz
+    count = jnp.int32(0)
+    for r in rows_sent:
+        for s in range(nnz):
+            picks[count] = r * nnz + s
+            count = count + ((ints[r, SENT] >> (ints[r, shift_lane(s)] + BAND)) & 1)
     copies = []
-    for side, arrays in enumerate(outs):
-        for n in range(BAND * nnz):
-            picks[side, n] = REACH * nnz
-        count = jnp.int32(0)
-        for q in range(BAND):
-            r = REACH + rows - BAND - 1 - q if side == 0 else REACH + BAND + q
-            for s in range(nnz):
-                picks[side, count] = r * nnz + s
-                count = count + ((ints[r, SENT] >> (ints[r, shift_lane(s)] + BAND)) & 1)
-        n = 0
-        for out in arrays:
-            for place in range(out.shape[0]):
-                copy = pltpu.make_async_copy(
-                    pool.at[pl.ds(picks[side, n], 1)], out.at[pl.ds(place, 1)], sem.at[side, n]
-                )
-                copy.start()
-                copies.append(copy)
-                n += 1
+    for n in range(out.shape[0]):
+        copy = pltpu.make_async_copy(
+            pool.at[pl.ds(picks[skip + n], 1)], out.at[pl.ds(n, 1)], sem.at[n]
+        )
+        copy.start()
+        copies.append(copy)
     return copies
 
 
+def in_pairs(count, step):
+    @pl.loop(0, count // 2)
+    def _(half):
+        step(2 * half)
+        step(2 * half + 1)
+
+
+def gram_row(dims, scale, ints, i, pool, gram, place):
+    pnz = dims[2]
+    blocks = products(dims, ints, REACH + i, range(dims[1]), TO_X, pool, pool)
+    for p, block in enumerate(blocks):
+        gram[place * pnz + p] = (block * scale).astype(gram.dtype)
+
+
+def update_row(dims, ints, i, pool, gram, target, place):
+    pnz = dims[2]
+    r = REACH + i
+    blocks = products(dims, ints, r, range(dims[1]), TO_GRAM, pool, gram)
+    for p, block in enumerate(blocks):
+        kept = pool[ints[r, TO_X + ints[r, want_lane(p)] + CENTRE]].astype(jnp.float32)
+        target[place * pnz + p] = (1.5 * kept - 0.5 * block).astype(target.dtype)
+
+
+def crossing(dims, upper):
+    rows, nnz, _ = dims
+    if upper:
+        spans = [(nnz - 1 - e, e + 1) for e in range(BAND)]
+        listed = [rows + e for e in range(BAND)] + [rows - BAND + e for e in range(BAND)]
+    else:
+        spans = [(0, BAND - e) for e in range(BAND)]
+        listed = [e - BAND for e in range(BAND)] + list(range(BAND))
+    return [(row, *span) for row, span in zip(listed, spans + spans)]
+
+
 def inner_kernel(
-    dims, scale, ints, x, out, up, down, up_rest, down_rest, pool, gram, picks, sems, pick_sems
+    dims, scale, ints, x, out, up, down, pool, gram, picks, sems, pick_sems
 ):
     rows, nnz, pnz = dims
     copies = begin(sems, [(x, pool, REACH * nnz)])
     clear(pool)
     finish(copies)
-    outs = ((up, up_rest), (down, down_rest))
-    listed = gather(dims, ints, pool, outs, picks, pick_sems)
-
-    @pl.loop(0, rows - 2 * BAND)
-    def _(i):
-        r = REACH + BAND + i
-        for p, block in enumerate(products(dims, ints, r, range(nnz), TO_X, pool, pool)):
-            gram[i * pnz + p] = (block * scale).astype(gram.dtype)
-
+    listed = []
+    for side, sent in enumerate((up, down)):
+        listed += gather(dims, ints, side, 0, pool, sent, picks.at[side], pick_sems.at[side])
+    in_pairs(rows - 2 * BAND, lambda n: gram_row(dims, scale, ints, BAND + n, pool, gram, n))
     finish(begin(sems, [(gram, out, 0)]) + listed)
 
 
 def near_kernel(
-    dims, scale, ints, x, low, high, inner, out, part, gram_part, pool, gram, done, kept_sums,
-    near_sums, sems
+    dims, scale, upper, ints, x, near, inner, *rest
 ):
+    if upper:
+        rest = rest[1:]
+    out, part, gram_part, lefts, sent, *rest = rest
+    pool, gram, done, kept_sums, near_sums, picks, sems, left_sems, pick_sems = rest
     rows, nnz, pnz = dims
+    half, many = rows // 2, near.shape[0]
     start = REACH * nnz
-    edge = BAND * pnz
-    own, near = x.shape[0], low.shape[0]
-    half = own // 2
+    mine = half * nnz
+    x_from = mine if upper else 0
+    near_at = start + 2 * mine if upper else start - many
     copies = begin(sems, [
-        (low, pool, start - near), (x.at[pl.ds(0, half)], pool, start),
-        (high, pool, start + own), (x.at[pl.ds(half, half)], pool, start + half),
-        (inner, gram, edge),
+        (near, pool, near_at), (x.at[pl.ds(x_from, mine)], pool, start + x_from),
+        (inner, gram, BAND * pnz),
     ])
     clear(pool)
     clear(gram)
-
-    def edge_grams(first_row, halo_row, place):
-        @pl.loop(0, BAND)
-        def _(e):
-            i = first_row + e
-            blocks = products(dims, ints, REACH + i, range(nnz), TO_X, pool, pool)
-            for p, block in enumerate(blocks):
-                gram[i * pnz + p] = (block * scale).astype(gram.dtype)
-
-        @pl.loop(0, BAND)
-        def _(e):
-            r = REACH + halo_row + e
-            blocks = products(dims, ints, r, range(nnz), TO_X, pool, pool)
-            for p, block in enumerate(blocks):
-                near_sums[(place + e) * pnz + p] = block
+    edge = rows - BAND if upper else 0
+    halo = rows if upper else -BAND
+    full = half if upper else BAND
+
+    def halo_row(n):
+        blocks = products(dims, ints, REACH + halo + n, range(nnz), TO_X, pool, pool)
+        for p, block in enumerate(blocks):
+            near_sums[n * pnz + p] = block
 
     finish(copies[:2])
-    edge_grams(0, -BAND, 0)
-    finish(copies[2:4])
-    edge_grams(rows - BAND, rows, BAND)
-    finish(copies[4:])
+    place, moves = 0, []
+    for row, slot, count in crossing(dims, upper):
+        moves.append((pool.at[pl.ds((REACH + row) * nnz + slot, count)], lefts, place))
+        place += count
+    laid = begin(left_sems, moves)
+    side, skip = 0 if upper else 1, BAND * nnz - sent.shape[0]
+    laid += gather(dims, ints, side, skip, pool, sent, picks, pick_sems)
+    in_pairs(BAND, halo_row)
     first = begin(sems.at[pl.ds(0, 1)], [(near_sums, gram_part, 0)])
-
-    def update(r, store):
-        blocks = products(dims, ints, r, range(nnz), TO_GRAM, pool, gram)
-        for p, block in enumerate(blocks):
-            kept = pool[ints[r, TO_X + ints[r, want_lane(p)] + CENTRE]].astype(jnp.float32)
-            store(p, 1.5 * kept - 0.5 * block)
-
-    @pl.loop(0, 2 * BAND)
-    def _(e):
-        def store(p, value):
-            kept_sums[e * pnz + p] = value
-
-        update(REACH + jnp.where(e < BAND, e, rows - 2 * BAND + e), store)
-
+    finish(copies[2:])
+    in_pairs(BAND, lambda n: gram_row(dims, scale, ints, edge + n, pool, gram, edge + n))
+    in_pairs(BAND, lambda n: update_row(dims, ints, edge + n, pool, gram, kept_sums, n))
     second = begin(sems.at[pl.ds(1, 1)], [(kept_sums, part, 0)])
-
-    @pl.loop(BAND, rows - BAND)
-    def _(i):
-        def store(p, value):
-            done[(i - BAND) * pnz + p] = value.astype(done.dtype)
-
-        update(REACH + i, store)
-
-    third = begin(sems.at[pl.ds(2, 1)], [(done, out, edge)])
-    finish(first + second + third)
+    in_pairs(half - BAND, lambda n: update_row(dims, ints, full + n, pool, gram, done, n))
+    third = begin(sems.at[pl.ds(2, 1)], [(done, out, full * pnz)])
+    finish(first + second + third + laid)
 
 
 def far_kernel(
-    dims, scale, ints, x, low, high, far_low, far_high, more, part, gram_part, unused, out, pool, far, gram, near_sums, kept_sums, done, sems
+    dims, scale, ints, left_low, left_high, far_low, far_high, more, part_low, part_high,
+    gram_low, gram_high, unused, out, left, far, gram, near_sums, kept_sums, done, sems
 ):
     rows, nnz, pnz = dims
-    near = low.shape[0]
-    own = x.shape[0]
-    start = BAND * nnz
-    edge = BAND * pnz
     first = far_low.shape[0]
     extra = more.shape[0] // 2
-    moves = [
+    edge = BAND * pnz
+    copies = begin(sems, [
+        (left_low, left, 0),
+        (left_high, left, left_low.shape[0]),
+        (far_low, far, 0),
+        (far_high, far, first + extra),
         (more.at[pl.ds(0, extra)], far, first),
         (more.at[pl.ds(extra, extra)], far, 2 * first + extra),
-        (far_low, far, 0),
-        (far_high, far, first + extra),
-        (low, pool, start - near),
-        (high, pool, start + own),
-        (x.at[pl.ds(0, near)], pool, start),
-        (x.at[pl.ds(own - near, near)], pool, start + own - near),
-    ]
-    copies = begin(sems, moves)
-    used = len(moves) + 4
-    late = begin(sems.at[pl.ds(len(moves), 4)], [
-        (half.at[pl.ds(e, edge)], target, e)
-        for half, target in ((gram_part, near_sums), (part, kept_sums))
-        for e in (0, edge)
     ])
+    late = begin(sems.at[pl.ds(len(copies), 4)], [
+        (gram_low, near_sums, 0), (gram_high, near_sums, edge),
+        (part_low, kept_sums, 0), (part_high, kept_sums, edge),
+    ])
+    used = len(copies) + len(late)
     clear(far)
     clear(gram)
     finish(copies)
-    offset = (REACH - BAND) * nnz
-
-    for e in range(2 * BAND):
-        if e % BAND == 0:
-            late[e // BAND].wait()
-        if e < BAND:
-            r, slots = REACH - BAND + e, range(0, BAND - e)
-        else:
-            r, slots = REACH + rows - BAND + e, range(nnz - 1 - (e - BAND), nnz)
-        blocks = products(dims, ints, r, slots, TO_FAR, pool, far, offset)
-        for p, block in enumerate(blocks):
-            n = e * pnz + p
-            gram[n] = ((near_sums[n] + block) * scale).astype(gram.dtype)
-
-    outgoing = []
-    for e in range(2 * BAND):
-        if e % BAND == 0:
-            late[2 + e // BAND].wait()
-        if e < BAND:
-            i, slots = e, range(0, BAND - e)
-        else:
-            i, slots = rows - 2 * BAND + e, range(nnz - 1 - (e - BAND), nnz)
-        blocks = products(dims, ints, REACH + i, slots, TO_HALO, pool, gram, offset)
-        for p, block in enumerate(blocks):
-            n = e * pnz + p
-            done[n] = (kept_sums[n] - 0.5 * block).astype(done.dtype)
-        outgoing += begin(
-            sems.at[pl.ds(used + e, 1)], [(done.at[pl.ds(e * pnz, pnz)], out, i * pnz)]
-        )
+    low_rows, high_rows = crossing(dims, False), crossing(dims, True)
+    place, tasks = 0, []
+    for row, slot, many in low_rows + high_rows:
+        tasks.append((row, range(slot, slot + many), (REACH + row) * nnz + slot - place))
+        place += many
+
+    def group(listed, table, right, at, store):
+        for e, (row, slots, base) in enumerate(listed):
+            blocks = products(dims, ints, REACH + row, slots, table, left, right, base)
+            for p, block in enumerate(blocks):
+                store(at + e * pnz + p, block)
+
+    def store_gram(n, block):
+        gram[n] = ((near_sums[n] + block) * scale).astype(gram.dtype)
+
+    def store_done(n, block):
+        done[n] = (kept_sums[n] - 0.5 * block).astype(done.dtype)
+
+    late[0].wait()
+    group(tasks[:BAND], TO_FAR, far, 0, store_gram)
+    late[1].wait()
+    group(tasks[2 * BAND:3 * BAND], TO_FAR, far, edge, store_gram)
+    late[2].wait()
+    group(tasks[BAND:2 * BAND], TO_HALO, gram, 0, store_done)
+    outgoing = begin(sems.at[pl.ds(used, 1)], [(done.at[pl.ds(0, edge)], out, 0)])
+    late[3].wait()
+    group(tasks[3 * BAND:], TO_HALO, gram, edge, store_done)
+    outgoing += begin(
+        sems.at[pl.ds(used + 1, 1)], [(done.at[pl.ds(edge, edge)], out, (rows - BAND) * pnz)]
+    )
     finish(outgoing)
 
 
@@ -431,20 +433,19 @@
 
     lists = pltpu.SMEM((2, 32), jnp.int32)
     remaining = most - first
-    inner, up, down, up_rest, down_rest = pl.pallas_call(
+    inner, up, down = pl.pallas_call(
         partial(inner_kernel, dims, scale),
         out_shape=[
-            shaped((rows - 2 * BAND) * pnz), shaped(first), shaped(first), shaped(remaining),
-            shaped(remaining),
+            shaped((rows - 2 * BAND) * pnz), shaped(first), shaped(first)
         ],
         in_specs=[smem, hbm],
-        out_specs=[hbm] * 5,
+        out_specs=[hbm] * 3,
         scratch_shapes=[
             scratch(padded * nnz + 1),
             scratch((rows - 2 * BAND) * pnz),
             lists,
             pltpu.SemaphoreType.DMA((1,)),
-            pltpu.SemaphoreType.DMA((2, most)),
+            pltpu.SemaphoreType.DMA((2, first)),
         ],
         compiler_params=settings(BIG),
         cost_estimate=cost((rows - 2 * BAND) * nnz * pnz, 200),
@@ -452,43 +453,49 @@
     far_low = lax.ppermute(up, AXES, forward)
     far_high = lax.ppermute(down, AXES, backward)
 
-    def near_step(low, high, inner):
+    lefts_count = sum(span[2] for span in crossing(dims, False))
+
+    def half_of_rows(upper, near_rows, *made):
         return pl.pallas_call(
-            partial(near_kernel, dims, scale),
+            partial(near_kernel, dims, scale, upper),
             out_shape=[
-                shaped(rows * pnz), shaped(edge, jnp.float32), shaped(edge, jnp.float32)
+                shaped(rows * pnz), shaped(edge // 2, jnp.float32),
+                shaped(edge // 2, jnp.float32), shaped(lefts_count), shaped(remaining),
             ],
-            in_specs=[smem] + [hbm] * 4,
-            out_specs=[hbm] * 3,
+            in_specs=[smem] + [hbm] * (3 + len(made)),
+            out_specs=[hbm] * 5,
+            input_output_aliases={4: 0} if made else {},
             scratch_shapes=[
                 scratch(padded * nnz + 1),
                 scratch(rows * pnz + 1),
-                scratch((rows - 2 * BAND) * pnz),
-                scratch(edge, jnp.float32),
-                scratch(edge, jnp.float32),
-                pltpu.SemaphoreType.DMA((5,)),
+                scratch((rows // 2 - BAND) * pnz),
+                scratch(edge // 2, jnp.float32),
+                scratch(edge // 2, jnp.float32),
+                pltpu.SMEM((32,), jnp.int32),
+                pltpu.SemaphoreType.DMA((3,)),
+                pltpu.SemaphoreType.DMA((2 * BAND,)),
+                pltpu.SemaphoreType.DMA((remaining,)),
             ],
             compiler_params=settings(BIG),
-            cost_estimate=cost((4 * BAND + rows) * nnz * pnz, 900),
-        )(ints, x, low, high, inner)
-
-    def step(many, up, down, low, high, inner):
-        blank = jnp.zeros((remaining - many,) + block, jnp.bfloat16)
-        more = [blank, blank]
-        if many:
-            more_low = lax.ppermute(up[:many], AXES, forward)
-            more_high = lax.ppermute(down[:many], AXES, backward)
-            more = [more_low, blank, more_high, blank]
-        return *near_step(low, high, inner), jnp.concatenate(more)
-
-    sizes = [n for n in range(remaining) if n <= STEPS] + [remaining]
-    out, part, gram_part, more = lax.switch(
-        sum((largest > first + n).astype(jnp.int32) for n in sizes[:-1]),
-        [partial(step, many) for many in sizes], up_rest, down_rest, low, high, inner,
-    )
+            cost_estimate=cost((2 * BAND + rows // 2) * nnz * pnz, 500),
+        )(ints, x, near_rows, inner, *made)
+
+    out, part_low, gram_low, left_low, down_rest = half_of_rows(False, low)
+    out, part_high, gram_high, left_high, up_rest = half_of_rows(True, high, out)
+
+    def none_more(up, down):
+        return jnp.zeros((2 * remaining,) + block, jnp.bfloat16)
+
+    def all_more(up, down):
+        return jnp.concatenate(
+            [lax.ppermute(up, AXES, forward), lax.ppermute(down, AXES, backward)]
+        )
+
+    more = lax.cond(largest > first, all_more, none_more, up_rest, down_rest)
 
     operands = [
-        ints, x, low, high, far_low, far_high, more, part, gram_part, out
+        ints, left_low, left_high, far_low, far_high, more, part_low, part_high, gram_low,
+        gram_high, out,
     ]
     out = pl.pallas_call(
         partial(far_kernel, dims, scale),
@@ -497,13 +504,13 @@
         out_specs=hbm,
         input_output_aliases={len(operands) - 1: 0},
         scratch_shapes=[
-            scratch((rows + 2 * BAND) * nnz),
+            scratch(2 * lefts_count),
             scratch(2 * most + 1),
             scratch(edge + 1),
             scratch(edge, jnp.float32),
             scratch(edge, jnp.float32),
             scratch(edge),
-            pltpu.SemaphoreType.DMA((12 + 2 * BAND,)),
+            pltpu.SemaphoreType.DMA((12,)),
         ],
         compiler_params=settings(BIG),
         cost_estimate=cost(2 * BAND * nnz * pnz, 600),

time: 81 us -> 72 us (0.89)
  starting transfers between devices: 18.1 us -> 10.1 us
  waiting for transfers between devices: 8.26 us -> 13.8 us
  between operations: 5.97 us -> 0.73 us
  other arithmetic: 1 us -> 0 us
    ppermute x1, waiting for transfers between devices: 0.01 us -> 9.33 us  [body(): far_high = lax.ppermute(down, AXES, backward)]
    ppermute x2 -> x0, starting transfers between devices: 8.15 us -> none  [the longest x1 6.5 us: step(): more_low = lax.ppermute(up[:many], AXES, forward)]
    ppermute x1, waiting for transfers between devices: 8.25 us -> 4.43 us  [body(): high = lax.ppermute(x[:near], AXES, backward)]
    pallas_call x1 -> x2, Pallas kernels: 18.2 us -> 20.2 us  [half_of_rows(): pl.pallas_call(partial(near_kernel, dims, scale, upper), out_shape=[shape...]
    unnamed x2 -> x6, local copies, waits for them, and re-layouts: 0.01 us -> 1.73 us
    pallas_call x1, Pallas kernels: 9.26 us -> 7.7 us  [body(): pl.pallas_call(partial(inner_kernel, dims, scale), out_shape=[shaped((row...]
    slice x1, local copies, waits for them, and re-layouts: 2.86 us -> 1.47 us  [body(): high = lax.ppermute(x[:near], AXES, backward)]
    concatenate x1 -> x0, other arithmetic: 1 us -> none  [step(): return (*near_step(low, high, inner), jnp.concatenate(more))]
  transfers between devices with their start and end apart: 6 -> 4, of which waited for: 1 -> 2; matrix products, arithmetic and copies ran while one was open for 4% -> 2% of each run, Pallas kernels for 37% -> 42%
where the time goes in v3:
time: 72 us; the launch traced here: 71.3 us
  Pallas kernels  37.3 us (52%)
  waiting for transfers between devices  13.8 us (19%)
  starting transfers between devices  10.1 us (14%)
  blocking collectives  4.89 us (7%)
  local copies, waits for them, and re-layouts  4.5 us (6%)
  between operations  0.73 us (1%)
    pallas_call x2, Pallas kernels, half_of_rows(): pl.pallas_call(partial(near_kernel, dims, scale, upper), out_shape=[shape...  20.2 us
    ppermute x1, waiting for transfers between devices, body(): far_high = lax.ppermute(down, AXES, backward)  9.33 us
    pallas_call x1, Pallas kernels, body(): pl.pallas_call(partial(inner_kernel, dims, scale), out_shape=[shaped((row...  7.7 us
    pallas_call x1, Pallas kernels, body(): pl.pallas_call(partial(far_kernel, dims, scale), out_shape=shaped(rows *...  7.58 us
    pmax x1, blocking collectives, body(): largest = lax.pmax(largest[0, 0], 'groups')  4.89 us
    ppermute x1, starting transfers between devices, body(): far_high = lax.ppermute(down, AXES, backward)  4.43 us
    ppermute x1, waiting for transfers between devices, body(): high = lax.ppermute(x[:near], AXES, backward)  4.43 us
    ppermute x1, starting transfers between devices, body(): low = lax.ppermute(x[rows * nnz - near:], AXES, forward)  3.08 us
  transfers between devices with their start and end apart: 4, of which 2 were waited for; matrix products, arithmetic and copies ran while one was open for 2% of the time, Pallas kernels for 42%

profile of v3, /device:TPU:0, one launch (start us, length us, event | category | flops | bytes accessed | tf_op | source)
XLA Modules:
  0.0 71.3 jit_solution(18031515264733751514)
XLA Ops:
  0.0 1.5 %fusion = (bf16[4,6,128,128]{3,2,1,0:T(8,128)(2,1)S(1)}, bf16[4,6,128,128]{3,2,1,0:T(8,128)(2,1)S(1)}) fusion(bf16[16,6,128,128]{3,2,1,0:T(8,128)(2,1)} %param.5), kind=kLoop, calls=%fused_computation.1 | loop fusion | bytes 3145728 | tf_op jit(solution)/shard_map/slice | solution.py:419
  1.5 3.1 %collective-permute-start.2 = (bf16[24,128,128]{2,1,0:T(8,128)(2,1)S(1)}, bf16[24,128,128]{2,1,0:T(8,128)(2,1)}, u32[]{:S(2)}, u32[]{:S(2)}) collective-permute-start(bf16[24,128,128]{2,1,0:T(8,128)(2,1)S(1)} %bitcast.12), channel_id=1, source_target_pairs={{0,1},{1,2},{2,3},{3,4},{4,5},{5,6},{6,7},{7,8},{8,9},{9,10},{10,1... | collective-permute-start | bytes 2359304 | tf_op jit(solution)/shard_map/ppermute | solution.py:418
  4.6 2.5 %collective-permute-start.3 = (bf16[24,128,128]{2,1,0:T(8,128)(2,1)S(1)}, bf16[24,128,128]{2,1,0:T(8,128)(2,1)S(1)}, u32[]{:S(2)}, u32[]{:S(2)}) collective-permute-start(bf16[24,128,128]{2,1,0:T(8,128)(2,1)S(1)} %bitcast.11), channel_id=1, source_target_pairs={{1,0},{2,1},{3,2},{4,3},{5,4},{6,5},{7,6},{8,7},{9,8},{10,9},{11,1... | collective-permute-start | bytes 2359304 | tf_op jit(solution)/shard_map/ppermute | solution.py:419
  7.0 1.9 %shard_map.37 = (s32[32,128]{1,0:T(8,128)}, s32[8,128]{1,0:T(8,128)}) custom-call(s32[1]{0:T(128)} %bitcast.me, s32[6,256]{1,0:T(8,128)} %bitcast.14, s32[10,256]{1,0:T(8,128)} %bitcast.13), custom_call_target="tpu_custom_call" | custom-call | tf_op jit(solution)/shard_map/pallas_call | solution.py:422
  8.9 7.7 %shard_map.38 = (bf16[80,128,128]{2,1,0:T(8,128)(2,1)}, bf16[16,128,128]{2,1,0:T(8,128)(2,1)}, bf16[16,128,128]{2,1,0:T(8,128)(2,1)}) custom-call(s32[32,128]{1,0:T(8,128)} %get-tuple-element.29.ints, bf16[96,128,128]{2,1,0:T(8,128)(2,1)} %bitcast.8), custom_call_target="tpu_custom_call" | custom-call | flops 2013265920 | bytes 6553600 | tf_op jit(solution)/shard_map/pallas_call | solution.py:436
  16.6 0.1 collective-permute-start.4
  16.7 4.4 %collective-permute-start.5 = (bf16[16,128,128]{2,1,0:T(8,128)(2,1)}, bf16[16,128,128]{2,1,0:T(8,128)(2,1)S(1)}, u32[]{:S(2)}, u32[]{:S(2)}) collective-permute-start(bf16[16,128,128]{2,1,0:T(8,128)(2,1)} %get-tuple-element.35), channel_id=1, source_target_pairs={{1,0},{2,1},{3,2},{4,3},{5,4},{6,5},{7,6},{8,7},{9,8},{10,9},{11,1... | collective-permute-start | bytes 1572872 | tf_op jit(solution)/shard_map/ppermute | solution.py:454
  21.1 1.2 %slice.19 = s32[1,1]{1,0:T(1,128)} slice(s32[8,128]{1,0:T(8,128)} %get-tuple-element.36), slice={[0:1], [0:1]} | slice | bytes 8 | tf_op jit(solution)/shard_map/slice | solution.py:432
  22.3 4.9 %pmax.7 = s32[]{:T(128)} all-reduce(s32[]{:T(128)} %bitcast.6), channel_id=1, replica_groups=mesh['groups'=2,'grid'=4,'rep'=4] {'groups'}, use_global_device_ids=true, to_apply=%region_0.0 | all-reduce | flops 1 | bytes 8 | tf_op jit(solution)/shard_map/pmax | solution.py:432
  27.9 0.0 collective-permute-done.2.near
  27.9 10.1 %shard_map.39 = (bf16[160,128,128]{2,1,0:T(8,128)(2,1)}, f32[40,128,128]{2,1,0:T(8,128)}, f32[40,128,128]{2,1,0:T(8,128)}, bf16[20,128,128]{2,1,0:T(8,128)(2,1)}, bf16[8,128,128]{2,1,0:T(8,128)(2,1)S(1)}) custom-call(s32[32,128]{1,0:T(8,128)} %get-tuple-element.29.ints, bf16[96,128,128]{2,1,0:T(8,128)(2,1)} %bitcast.9, ...), custom_call_target="tpu_custom_call" | custom-call | flops 4026531840 | bytes 16384000 | tf_op jit(solution)/shard_map/pallas_call | solution.py:459
  38.0 4.4 %collective-permute-done.3.near = bf16[24,128,128]{2,1,0:T(8,128)(2,1)S(1)} collective-permute-done((bf16[24,128,128]{2,1,0:T(8,128)(2,1)S(1)}, bf16[24,128,128]{2,1,0:T(8,128)(2,1)S(1)}, u32[]{:S(2)}, u32[]{:S(2)}) %collective-permute-start.3) | collective-permute-done | bytes 786464 | tf_op jit(solution)/shard_map/ppermute | solution.py:419
  42.4 0.0 copy-start.2
  42.4 0.9 %copy-done.2 = bf16[24,128,128]{2,1,0:T(8,128)(2,1)} copy-done((bf16[24,128,128]{2,1,0:T(8,128)(2,1)}, bf16[24,128,128]{2,1,0:T(8,128)(2,1)S(1)}, u32[]{:S(2)}) %copy-start.2) | copy-done | bytes 786456
  43.3 10.1 %shard_map.40 = (bf16[160,128,128]{2,1,0:T(8,128)(2,1)}, f32[40,128,128]{2,1,0:T(8,128)}, f32[40,128,128]{2,1,0:T(8,128)}, bf16[20,128,128]{2,1,0:T(8,128)(2,1)}, bf16[8,128,128]{2,1,0:T(8,128)(2,1)S(1)}) custom-call(s32[32,128]{1,0:T(8,128)} %get-tuple-element.29.ints, bf16[96,128,128]{2,1,0:T(8,128)(2,1)} %bitcast.10, ...), custom_call_target="tpu_custom_call", output_to_operand_aliasing={{0}: (4, {})} | custom-call | flops 4026531840 | bytes 16384000 | tf_op jit(solution)/shard_map/pallas_call | solution.py:459
  53.4 0.1 conditional.1
  53.4 0.1 broadcast.2
  53.5 0.0 collective-permute-done.4.far_low
  53.5 0.0 copy-start
  53.6 9.3 %collective-permute-done.5.far_high = bf16[16,128,128]{2,1,0:T(8,128)(2,1)S(1)} collective-permute-done((bf16[16,128,128]{2,1,0:T(8,128)(2,1)}, bf16[16,128,128]{2,1,0:T(8,128)(2,1)S(1)}, u32[]{:S(2)}, u32[]{:S(2)}) %collective-permute-start.5) | collective-permute-done | bytes 524320 | tf_op jit(solution)/shard_map/ppermute | solution.py:454
  62.9 0.0 copy-start.1
  62.9 0.0 copy-done
  62.9 0.8 %copy-done.1 = bf16[16,128,128]{2,1,0:T(8,128)(2,1)} copy-done((bf16[16,128,128]{2,1,0:T(8,128)(2,1)}, bf16[16,128,128]{2,1,0:T(8,128)(2,1)S(1)}, u32[]{:S(2)}) %copy-start.1) | copy-done | bytes 524312
  63.7 7.6 %shard_map.41 = bf16[160,128,128]{2,1,0:T(8,128)(2,1)} custom-call(s32[32,128]{1,0:T(8,128)} %get-tuple-element.29.ints, bf16[20,128,128]{2,1,0:T(8,128)(2,1)} %get-tuple-element.31.left_low, bf16[20,128,128]{2,1,0:T(8,128)(2,1)} %get-tuple-element.33.left_high, bf16[16,128,128]{2,1,0:T(8,128)(2,1)} %copy-done, ...), custom_call_target="tpu_custom_call", output_to_operand_aliasing={{}: (10, {})} | custom-call | flops 2013265920 | bytes 19660800 | tf_op jit(solution)/shard_map/pallas_call | solution.py:500
Async XLA Ops:
  1.5 26.4 %collective-permute-start.2 = (bf16[24,128,128]{2,1,0:T(8,128)(2,1)S(1)}, bf16[24,128,128]{2,1,0:T(8,128)(2,1)}, u32[]{:S(2)}, u32[]{:S(2)}) collective-permute-start(bf16[24,128,128]{2,1,0:T(8,128)(2,1)S(1)} %bitcast.12), channel_id=1, source_target_pairs={{0,1},{1,2},{2,3},{3,4},{4,5},{5,6},{6,7},{7,8},{8,9},{9,10},{10,1... | collective-permute-start | bytes 2359304 | tf_op jit(solution)/shard_map/ppermute | solution.py:418
  4.6 37.8 %collective-permute-start.3 = (bf16[24,128,128]{2,1,0:T(8,128)(2,1)S(1)}, bf16[24,128,128]{2,1,0:T(8,128)(2,1)S(1)}, u32[]{:S(2)}, u32[]{:S(2)}) collective-permute-start(bf16[24,128,128]{2,1,0:T(8,128)(2,1)S(1)} %bitcast.11), channel_id=1, source_target_pairs={{1,0},{2,1},{3,2},{4,3},{5,4},{6,5},{7,6},{8,7},{9,8},{10,9},{11,1... | collective-permute-start | bytes 2359304 | tf_op jit(solution)/shard_map/ppermute | solution.py:419
  16.6 36.9 %collective-permute-start.4 = (bf16[16,128,128]{2,1,0:T(8,128)(2,1)}, bf16[16,128,128]{2,1,0:T(8,128)(2,1)S(1)}, u32[]{:S(2)}, u32[]{:S(2)}) collective-permute-start(bf16[16,128,128]{2,1,0:T(8,128)(2,1)} %get-tuple-element.34), channel_id=1, source_target_pairs={{0,1},{1,2},{2,3},{3,4},{4,5},{5,6},{6,7},{7,8},{8,9},{9,10},{10,1... | collective-permute-start | bytes 1572872 | tf_op jit(solution)/shard_map/ppermute | solution.py:453
  16.7 46.2 %collective-permute-start.5 = (bf16[16,128,128]{2,1,0:T(8,128)(2,1)}, bf16[16,128,128]{2,1,0:T(8,128)(2,1)S(1)}, u32[]{:S(2)}, u32[]{:S(2)}) collective-permute-start(bf16[16,128,128]{2,1,0:T(8,128)(2,1)} %get-tuple-element.35), channel_id=1, source_target_pairs={{1,0},{2,1},{3,2},{4,3},{5,4},{6,5},{7,6},{8,7},{9,8},{10,9},{11,1... | collective-permute-start | bytes 1572872 | tf_op jit(solution)/shard_map/ppermute | solution.py:454
  42.4 0.9 %copy-start.2 = (bf16[24,128,128]{2,1,0:T(8,128)(2,1)}, bf16[24,128,128]{2,1,0:T(8,128)(2,1)S(1)}, u32[]{:S(2)}) copy-start(bf16[24,128,128]{2,1,0:T(8,128)(2,1)S(1)} %collective-permute-done.3.near) | copy-start | bytes 2359300
  53.5 9.3 %copy-start = (bf16[16,128,128]{2,1,0:T(8,128)(2,1)}, bf16[16,128,128]{2,1,0:T(8,128)(2,1)S(1)}, u32[]{:S(2)}) copy-start(bf16[16,128,128]{2,1,0:T(8,128)(2,1)S(1)} %collective-permute-done.4.far_low) | copy-start | bytes 1572868
  62.9 0.8 %copy-start.1 = (bf16[16,128,128]{2,1,0:T(8,128)(2,1)}, bf16[16,128,128]{2,1,0:T(8,128)(2,1)S(1)}, u32[]{:S(2)}) copy-start(bf16[16,128,128]{2,1,0:T(8,128)(2,1)S(1)} %collective-permute-done.5.far_high) | copy-start | bytes 1572868

commit v4 on v3

--- a/solution.py
+++ b/solution.py
@@ -13,7 +13,7 @@
 AXES = ("grid", "rep")
 MIB = 1024 * 1024
 FIRST = 16
-BIG = 60
+BIG = 62
 TO_X, TO_GRAM, TO_FAR, TO_HALO = 0, 32, 64, 96
 LANES = 128
 SPARE = 25
@@ -200,6 +200,12 @@
     return copies
 
 
+def table_copy(source, ints, sem):
+    copy = pltpu.make_async_copy(source, ints, sem.at[0])
+    copy.start()
+    return copy
+
+
 def finish(copies):
     for copy in copies:
         copy.wait()
@@ -261,10 +267,10 @@
 
 
 def inner_kernel(
-    dims, scale, ints, x, out, up, down, pool, gram, picks, sems, pick_sems
+    dims, scale, table, x, out, up, down, ints, pool, gram, picks, table_sem, sems, pick_sems
 ):
     rows, nnz, pnz = dims
-    copies = begin(sems, [(x, pool, REACH * nnz)])
+    copies = [table_copy(table, ints, table_sem)] + begin(sems, [(x, pool, REACH * nnz)])
     clear(pool)
     finish(copies)
     listed = []
@@ -274,20 +280,16 @@
     finish(begin(sems, [(gram, out, 0)]) + listed)
 
 
-def near_kernel(
-    dims, scale, upper, ints, x, near, inner, *rest
-):
-    if upper:
-        rest = rest[1:]
-    out, part, gram_part, lefts, sent, *rest = rest
-    pool, gram, done, kept_sums, near_sums, picks, sems, left_sems, pick_sems = rest
+def near_kernel(dims, scale, upper, table, x, near, inner, *rest):
+    out, part, gram_part, sent, lefts, ints, *scratch = rest[-16:]
+    pool, gram, done, own_sums, near_sums, picks, table_sem, sems, pick_sems, left_sems = scratch
     rows, nnz, pnz = dims
     half, many = rows // 2, near.shape[0]
     start = REACH * nnz
     mine = half * nnz
     x_from = mine if upper else 0
     near_at = start + 2 * mine if upper else start - many
-    copies = begin(sems, [
+    copies = [table_copy(table, ints, table_sem)] + begin(sems, [
         (near, pool, near_at), (x.at[pl.ds(x_from, mine)], pool, start + x_from),
         (inner, gram, BAND * pnz),
     ])
@@ -300,81 +302,99 @@
     def halo_row(n):
         blocks = products(dims, ints, REACH + halo + n, range(nnz), TO_X, pool, pool)
         for p, block in enumerate(blocks):
-            near_sums[n * pnz + p] = block
-
-    finish(copies[:2])
+            near_sums[n * pnz + p] = block.astype(near_sums.dtype)
+
+    def edge_row(n):
+        blocks = products(dims, ints, REACH + edge + n, range(nnz), TO_GRAM, pool, gram)
+        for p, block in enumerate(blocks):
+            own_sums[n * pnz + p] = block.astype(own_sums.dtype)
+
+    finish(copies[:3])
+    side, skip = 0 if upper else 1, BAND * nnz - sent.shape[0]
+    laid = gather(dims, ints, side, skip, pool, sent, picks, pick_sems)
     place, moves = 0, []
-    for row, slot, count in crossing(dims, upper):
+    for row, slot, count in crossing(dims, upper)[:BAND]:
         moves.append((pool.at[pl.ds((REACH + row) * nnz + slot, count)], lefts, place))
         place += count
-    laid = begin(left_sems, moves)
-    side, skip = 0 if upper else 1, BAND * nnz - sent.shape[0]
-    laid += gather(dims, ints, side, skip, pool, sent, picks, pick_sems)
+    laid += begin(left_sems, moves)
     in_pairs(BAND, halo_row)
     first = begin(sems.at[pl.ds(0, 1)], [(near_sums, gram_part, 0)])
-    finish(copies[2:])
+    finish(copies[3:])
     in_pairs(BAND, lambda n: gram_row(dims, scale, ints, edge + n, pool, gram, edge + n))
-    in_pairs(BAND, lambda n: update_row(dims, ints, edge + n, pool, gram, kept_sums, n))
-    second = begin(sems.at[pl.ds(1, 1)], [(kept_sums, part, 0)])
+    in_pairs(BAND, edge_row)
+    second = begin(sems.at[pl.ds(1, 1)], [(own_sums, part, 0)])
     in_pairs(half - BAND, lambda n: update_row(dims, ints, full + n, pool, gram, done, n))
     third = begin(sems.at[pl.ds(2, 1)], [(done, out, full * pnz)])
     finish(first + second + third + laid)
 
 
 def far_kernel(
-    dims, scale, ints, left_low, left_high, far_low, far_high, more, part_low, part_high,
-    gram_low, gram_high, unused, out, left, far, gram, near_sums, kept_sums, done, sems
+    dims, scale, table, x, left_low, left_high, far_low, far_high, more_low, more_high, gram_low, gram_high,
+    part_low, part_high, unused, out, ints, pool, far, gram, near_sums, own_sums, done, table_sem,
+    sems
 ):
     rows, nnz, pnz = dims
-    first = far_low.shape[0]
-    extra = more.shape[0] // 2
+    first, near, own = far_low.shape[0], BAND * nnz, x.shape[0]
     edge = BAND * pnz
-    copies = begin(sems, [
-        (left_low, left, 0),
-        (left_high, left, left_low.shape[0]),
-        (far_low, far, 0),
-        (far_high, far, first + extra),
-        (more.at[pl.ds(0, extra)], far, first),
-        (more.at[pl.ds(extra, extra)], far, 2 * first + extra),
+    start = REACH * nnz
+    moves = [
+        (far_low, far, 0), (more_low, far, first),
+        (far_high, far, near), (more_high, far, near + first),
+    ]
+    for upper, lefts in ((False, left_low), (True, left_high)):
+        place = 0
+        for row, slot, many in crossing(dims, upper)[:BAND]:
+            moves.append((lefts.at[pl.ds(place, many)], pool, (REACH + row) * nnz + slot))
+            place += many
+    early = [table_copy(table, ints, table_sem)] + begin(sems, moves)
+    late = begin(sems.at[pl.ds(len(moves), 6)], [
+        (gram_low, near_sums, 0), (gram_high, near_sums, edge),
+        (x.at[pl.ds(0, near)], pool, start), (part_low, own_sums, 0),
+        (x.at[pl.ds(own - near, near)], pool, start + own - near), (part_high, own_sums, edge),
     ])
-    late = begin(sems.at[pl.ds(len(copies), 4)], [
-        (gram_low, near_sums, 0), (gram_high, near_sums, edge),
-        (part_low, kept_sums, 0), (part_high, kept_sums, edge),
-    ])
-    used = len(copies) + len(late)
+    used = len(moves) + len(late)
+    clear(pool)
     clear(far)
     clear(gram)
-    finish(copies)
-    low_rows, high_rows = crossing(dims, False), crossing(dims, True)
-    place, tasks = 0, []
-    for row, slot, many in low_rows + high_rows:
-        tasks.append((row, range(slot, slot + many), (REACH + row) * nnz + slot - place))
-        place += many
-
-    def group(listed, table, right, at, store):
-        for e, (row, slots, base) in enumerate(listed):
-            blocks = products(dims, ints, REACH + row, slots, table, left, right, base)
+    finish(early)
+
+    def far_terms(upper):
+        for e, (row, slot, many) in enumerate(crossing(dims, upper)[:BAND]):
+            slots = range(slot, slot + many)
+            blocks = products(dims, ints, REACH + row, slots, TO_FAR, pool, far)
             for p, block in enumerate(blocks):
-                store(at + e * pnz + p, block)
-
-    def store_gram(n, block):
-        gram[n] = ((near_sums[n] + block) * scale).astype(gram.dtype)
-
-    def store_done(n, block):
-        done[n] = (kept_sums[n] - 0.5 * block).astype(done.dtype)
-
-    late[0].wait()
-    group(tasks[:BAND], TO_FAR, far, 0, store_gram)
-    late[1].wait()
-    group(tasks[2 * BAND:3 * BAND], TO_FAR, far, edge, store_gram)
-    late[2].wait()
-    group(tasks[BAND:2 * BAND], TO_HALO, gram, 0, store_done)
-    outgoing = begin(sems.at[pl.ds(used, 1)], [(done.at[pl.ds(0, edge)], out, 0)])
-    late[3].wait()
-    group(tasks[3 * BAND:], TO_HALO, gram, edge, store_done)
-    outgoing += begin(
-        sems.at[pl.ds(used + 1, 1)], [(done.at[pl.ds(edge, edge)], out, (rows - BAND) * pnz)]
-    )
+                n = (upper * BAND + e) * pnz + p
+                whole = near_sums[n].astype(jnp.float32) + block
+                gram[n] = (whole * scale).astype(gram.dtype)
+
+    def halo_terms(upper, places):
+        for e in places:
+            row, slot, many = crossing(dims, upper)[BAND + e]
+            r = REACH + row
+            slots = range(slot, slot + many)
+            blocks = products(dims, ints, r, slots, TO_HALO, pool, gram)
+            for p, block in enumerate(blocks):
+                n = (upper * BAND + e) * pnz + p
+                kept = pool[ints[r, TO_X + ints[r, want_lane(p)] + CENTRE]].astype(jnp.float32)
+                whole = own_sums[n].astype(jnp.float32) + block
+                done[n] = (1.5 * kept - 0.5 * whole).astype(done.dtype)
+        at, many = (upper * BAND + places[0]) * pnz, len(places) * pnz
+        place = (places[0] + (rows - BAND if upper else 0)) * pnz
+        return begin(
+            sems.at[pl.ds(used + 2 * upper + places[0] // 2, 1)],
+            [(done.at[pl.ds(at, many)], out, place)],
+        )
+
+    finish(late[:1])
+    far_terms(False)
+    finish(late[1:2])
+    far_terms(True)
+    finish(late[2:4])
+    half = BAND // 2
+    outgoing = halo_terms(False, range(BAND))
+    finish(late[4:])
+    outgoing += halo_terms(True, range(half, BAND))
+    outgoing += halo_terms(True, range(half))
     finish(outgoing)
 
 
@@ -432,18 +452,21 @@
     largest = lax.pmax(largest[0, 0], "groups")
 
     lists = pltpu.SMEM((2, 32), jnp.int32)
+    table = pltpu.SMEM((padded, LANES), jnp.int32)
     remaining = most - first
     inner, up, down = pl.pallas_call(
         partial(inner_kernel, dims, scale),
         out_shape=[
             shaped((rows - 2 * BAND) * pnz), shaped(first), shaped(first)
         ],
-        in_specs=[smem, hbm],
+        in_specs=[hbm, hbm],
         out_specs=[hbm] * 3,
         scratch_shapes=[
+            table,
             scratch(padded * nnz + 1),
             scratch((rows - 2 * BAND) * pnz),
             lists,
+            pltpu.SemaphoreType.DMA((1,)),
             pltpu.SemaphoreType.DMA((1,)),
             pltpu.SemaphoreType.DMA((2, first)),
         ],
@@ -453,67 +476,70 @@
     far_low = lax.ppermute(up, AXES, forward)
     far_high = lax.ppermute(down, AXES, backward)
 
-    lefts_count = sum(span[2] for span in crossing(dims, False))
+    half_edge = BAND * pnz
+    lefts_count = sum(span[2] for span in crossing(dims, False)[:BAND])
 
     def half_of_rows(upper, near_rows, *made):
         return pl.pallas_call(
             partial(near_kernel, dims, scale, upper),
             out_shape=[
-                shaped(rows * pnz), shaped(edge // 2, jnp.float32),
-                shaped(edge // 2, jnp.float32), shaped(lefts_count), shaped(remaining),
+                shaped(rows * pnz), shaped(half_edge), shaped(half_edge), shaped(remaining),
+                shaped(lefts_count),
             ],
-            in_specs=[smem] + [hbm] * (3 + len(made)),
+            in_specs=[hbm] * (4 + len(made)),
             out_specs=[hbm] * 5,
             input_output_aliases={4: 0} if made else {},
             scratch_shapes=[
+                table,
                 scratch(padded * nnz + 1),
                 scratch(rows * pnz + 1),
                 scratch((rows // 2 - BAND) * pnz),
-                scratch(edge // 2, jnp.float32),
-                scratch(edge // 2, jnp.float32),
+                scratch(half_edge),
+                scratch(half_edge),
                 pltpu.SMEM((32,), jnp.int32),
+                pltpu.SemaphoreType.DMA((1,)),
                 pltpu.SemaphoreType.DMA((3,)),
-                pltpu.SemaphoreType.DMA((2 * BAND,)),
                 pltpu.SemaphoreType.DMA((remaining,)),
+                pltpu.SemaphoreType.DMA((BAND,)),
             ],
             compiler_params=settings(BIG),
             cost_estimate=cost((2 * BAND + rows // 2) * nnz * pnz, 500),
         )(ints, x, near_rows, inner, *made)
 
-    out, part_low, gram_low, left_low, down_rest = half_of_rows(False, low)
-    out, part_high, gram_high, left_high, up_rest = half_of_rows(True, high, out)
-
-    def none_more(up, down):
-        return jnp.zeros((2 * remaining,) + block, jnp.bfloat16)
-
-    def all_more(up, down):
-        return jnp.concatenate(
-            [lax.ppermute(up, AXES, forward), lax.ppermute(down, AXES, backward)]
-        )
-
-    more = lax.cond(largest > first, all_more, none_more, up_rest, down_rest)
+    out, part_low, gram_low, down_rest, left_low = half_of_rows(False, low)
+    out, part_high, gram_high, up_rest, left_high = half_of_rows(True, high, out)
+
+    def send_rest(state):
+        _, up, down = state
+        return False, lax.ppermute(up, AXES, forward), lax.ppermute(down, AXES, backward)
+
+    _, more_low, more_high = lax.while_loop(
+        lambda state: state[0], send_rest, (largest > first, up_rest, down_rest)
+    )
 
     operands = [
-        ints, left_low, left_high, far_low, far_high, more, part_low, part_high, gram_low,
-        gram_high, out,
+        ints, x, left_low, left_high, far_low, far_high, more_low, more_high, gram_low, gram_high, part_low,
+        part_high, out,
     ]
     out = pl.pallas_call(
         partial(far_kernel, dims, scale),
         out_shape=shaped(rows * pnz),
-        in_specs=[smem] + [hbm] * (len(operands) - 1),
+        in_specs=[hbm] * len(operands),
         out_specs=hbm,
         input_output_aliases={len(operands) - 1: 0},
         scratch_shapes=[
-            scratch(2 * lefts_count),
+            table,
+            scratch(padded * nnz + 1),
             scratch(2 * most + 1),
             scratch(edge + 1),
-            scratch(edge, jnp.float32),
-            scratch(edge, jnp.float32),
             scratch(edge),
-            pltpu.SemaphoreType.DMA((12,)),
+            scratch(edge),
+            scratch(edge),
+            pltpu.SemaphoreType.DMA((1,)),
+            pltpu.SemaphoreType.DMA((14 + 2 * BAND,)),
         ],
         compiler_params=settings(BIG),
-        cost_estimate=cost(2 * BAND * nnz * pnz, 600),
+        cost_estimate=cost(2 * BAND * nnz * pnz, 400),
     )(*operands)
     return out.reshape(rows, pnz, size, size)
 

time: 72 us -> 69.9 us (0.971)
  Pallas kernels: 37.3 us -> 32.9 us
  waiting for transfers between devices: 13.8 us -> 17.8 us
  local copies, waits for them, and re-layouts: 4.5 us -> 2.81 us
    pallas_call x2, Pallas kernels: 20.2 us -> 18.1 us  [half_of_rows(): pl.pallas_call(partial(near_kernel, dims, scale, upper), out_shape=[shape...]
    ppermute x1, waiting for transfers between devices: 4.43 us -> 6.35 us  [body(): high = lax.ppermute(x[:near], AXES, backward)]
    unnamed x6 -> x0, local copies, waits for them, and re-layouts: 1.73 us -> none
    pallas_call x1, Pallas kernels: 7.58 us -> 6.13 us  [body(): pl.pallas_call(partial(far_kernel, dims, scale), out_shape=shaped(rows *...]
    ppermute x1, waiting for transfers between devices: 0.01 us -> 1.07 us  [body(): far_low = lax.ppermute(up, AXES, forward)]
    ppermute x1, waiting for transfers between devices: 9.33 us -> 10.4 us  [body(): far_high = lax.ppermute(down, AXES, backward)]
    pallas_call x1, Pallas kernels: 7.7 us -> 6.88 us  [body(): pl.pallas_call(partial(inner_kernel, dims, scale), out_shape=[shaped((row...]
  transfers between devices with their start and end apart: 4 -> 4, of which waited for: 2 -> 3; matrix products, arithmetic and copies ran while one was open for 2% -> 2% of each run, Pallas kernels for 42% -> 39%
where the time goes in v4:
time: 69.9 us; the launch traced here: 69.2 us
  Pallas kernels  32.9 us (47%)
  waiting for transfers between devices  17.8 us (25%)
  starting transfers between devices  10.1 us (14%)
  blocking collectives  4.89 us (7%)
  local copies, waits for them, and re-layouts  2.81 us (4%)
  between operations  0.71 us (1%)
    pallas_call x2, Pallas kernels, half_of_rows(): pl.pallas_call(partial(near_kernel, dims, scale, upper), out_shape=[shape...  18.1 us
    ppermute x1, waiting for transfers between devices, body(): far_high = lax.ppermute(down, AXES, backward)  10.4 us
    pallas_call x1, Pallas kernels, body(): pl.pallas_call(partial(inner_kernel, dims, scale), out_shape=[shaped((row...  6.88 us
    ppermute x1, waiting for transfers between devices, body(): high = lax.ppermute(x[:near], AXES, backward)  6.35 us
    pallas_call x1, Pallas kernels, body(): pl.pallas_call(partial(far_kernel, dims, scale), out_shape=shaped(rows *...  6.13 us
    pmax x1, blocking collectives, body(): largest = lax.pmax(largest[0, 0], 'groups')  4.89 us
    ppermute x1, starting transfers between devices, body(): far_high = lax.ppermute(down, AXES, backward)  4.43 us
    ppermute x1, starting transfers between devices, body(): low = lax.ppermute(x[rows * nnz - near:], AXES, forward)  3.08 us
  transfers between devices with their start and end apart: 4, of which 3 were waited for; matrix products, arithmetic and copies ran while one was open for 2% of the time, Pallas kernels for 39%

profile of v4, /device:TPU:0, one launch (start us, length us, event | category | flops | bytes accessed | tf_op | source)
XLA Modules:
  0.0 69.2 jit_solution(1048849930703263587)
XLA Ops:
  0.0 1.5 %fusion = (bf16[4,6,128,128]{3,2,1,0:T(8,128)(2,1)S(1)}, bf16[4,6,128,128]{3,2,1,0:T(8,128)(2,1)S(1)}) fusion(bf16[16,6,128,128]{3,2,1,0:T(8,128)(2,1)} %param.5), kind=kLoop, calls=%fused_computation | loop fusion | bytes 3145728 | tf_op jit(solution)/shard_map/slice | solution.py:439
  1.5 3.1 %collective-permute-start.2 = (bf16[24,128,128]{2,1,0:T(8,128)(2,1)S(1)}, bf16[24,128,128]{2,1,0:T(8,128)(2,1)}, u32[]{:S(2)}, u32[]{:S(2)}) collective-permute-start(bf16[24,128,128]{2,1,0:T(8,128)(2,1)S(1)} %bitcast.13), channel_id=1, source_target_pairs={{0,1},{1,2},{2,3},{3,4},{4,5},{5,6},{6,7},{7,8},{8,9},{9,10},{10,1... | collective-permute-start | bytes 2359304 | tf_op jit(solution)/shard_map/ppermute | solution.py:438
  4.6 2.5 %collective-permute-start.3 = (bf16[24,128,128]{2,1,0:T(8,128)(2,1)S(1)}, bf16[24,128,128]{2,1,0:T(8,128)(2,1)}, u32[]{:S(2)}, u32[]{:S(2)}) collective-permute-start(bf16[24,128,128]{2,1,0:T(8,128)(2,1)S(1)} %bitcast.12), channel_id=1, source_target_pairs={{1,0},{2,1},{3,2},{4,3},{5,4},{6,5},{7,6},{8,7},{9,8},{10,9},{11,1... | collective-permute-start | bytes 2359304 | tf_op jit(solution)/shard_map/ppermute | solution.py:439
  7.1 1.9 %shard_map.37 = (s32[32,128]{1,0:T(8,128)}, s32[8,128]{1,0:T(8,128)}) custom-call(s32[1]{0:T(128)} %bitcast.me, s32[6,256]{1,0:T(8,128)} %bitcast.15, s32[10,256]{1,0:T(8,128)} %bitcast.14), custom_call_target="tpu_custom_call" | custom-call | tf_op jit(solution)/shard_map/pallas_call | solution.py:442
  9.0 6.9 %shard_map.38 = (bf16[80,128,128]{2,1,0:T(8,128)(2,1)}, bf16[16,128,128]{2,1,0:T(8,128)(2,1)}, bf16[16,128,128]{2,1,0:T(8,128)(2,1)}) custom-call(s32[32,128]{1,0:T(8,128)} %get-tuple-element.37.table, bf16[96,128,128]{2,1,0:T(8,128)(2,1)} %bitcast.8), custom_call_target="tpu_custom_call" | custom-call | flops 2013265920 | bytes 6553600 | tf_op jit(solution)/shard_map/pallas_call | solution.py:457
  15.9 0.1 collective-permute-start.4
  15.9 4.4 %collective-permute-start.5 = (bf16[16,128,128]{2,1,0:T(8,128)(2,1)}, bf16[16,128,128]{2,1,0:T(8,128)(2,1)}, u32[]{:S(2)}, u32[]{:S(2)}) collective-permute-start(bf16[16,128,128]{2,1,0:T(8,128)(2,1)} %get-tuple-element.43), channel_id=1, source_target_pairs={{1,0},{2,1},{3,2},{4,3},{5,4},{6,5},{7,6},{8,7},{9,8},{10,9},{11,1... | collective-permute-start | bytes 1572872 | tf_op jit(solution)/shard_map/ppermute | solution.py:477
  20.4 1.3 %slice.19 = s32[1,1]{1,0:T(1,128)} slice(s32[8,128]{1,0:T(8,128)} %get-tuple-element.44), slice={[0:1], [0:1]} | slice | bytes 8 | tf_op jit(solution)/shard_map/slice | solution.py:452
  21.6 4.9 %pmax.7 = s32[]{:T(128)} all-reduce(s32[]{:T(128)} %bitcast.6), channel_id=1, replica_groups=mesh['groups'=2,'grid'=4,'rep'=4] {'groups'}, use_global_device_ids=true, to_apply=%region_0.0 | all-reduce | flops 1 | bytes 8 | tf_op jit(solution)/shard_map/pmax | solution.py:452
  27.2 0.0 collective-permute-done.2.near
  27.2 9.0 %shard_map.39 = (bf16[160,128,128]{2,1,0:T(8,128)(2,1)}, bf16[40,128,128]{2,1,0:T(8,128)(2,1)}, bf16[40,128,128]{2,1,0:T(8,128)(2,1)}, bf16[8,128,128]{2,1,0:T(8,128)(2,1)S(1)}, bf16[10,128,128]{2,1,0:T(8,128)(2,1)}) custom-call(s32[32,128]{1,0:T(8,128)} %get-tuple-element.37.table, bf16[96,128,128]{2,1,0:T(8,128)(2,1)} %bitcast.9, ...), custom_call_target="tpu_custom_call" | custom-call | flops 4026531840 | bytes 16384000 | tf_op jit(solution)/shard_map/pallas_call | solution.py:483
  36.2 6.4 %collective-permute-done.3.near = bf16[24,128,128]{2,1,0:T(8,128)(2,1)} collective-permute-done((bf16[24,128,128]{2,1,0:T(8,128)(2,1)S(1)}, bf16[24,128,128]{2,1,0:T(8,128)(2,1)}, u32[]{:S(2)}, u32[]{:S(2)}) %collective-permute-start.3) | collective-permute-done | bytes 786464 | tf_op jit(solution)/shard_map/ppermute | solution.py:439
  42.6 9.0 %shard_map.40 = (bf16[160,128,128]{2,1,0:T(8,128)(2,1)}, bf16[40,128,128]{2,1,0:T(8,128)(2,1)}, bf16[40,128,128]{2,1,0:T(8,128)(2,1)}, bf16[8,128,128]{2,1,0:T(8,128)(2,1)S(1)}, bf16[10,128,128]{2,1,0:T(8,128)(2,1)}) custom-call(s32[32,128]{1,0:T(8,128)} %get-tuple-element.37.table, bf16[96,128,128]{2,1,0:T(8,128)(2,1)} %bitcast.10, ...), custom_call_target="tpu_custom_call", output_to_operand_aliasing={{0}: (4, {})} | custom-call | flops 4026531840 | bytes 16384000 | tf_op jit(solution)/shard_map/pallas_call | solution.py:483
  51.6 1.1 %collective-permute-done.4.far_low = bf16[16,128,128]{2,1,0:T(8,128)(2,1)} collective-permute-done((bf16[16,128,128]{2,1,0:T(8,128)(2,1)}, bf16[16,128,128]{2,1,0:T(8,128)(2,1)}, u32[]{:S(2)}, u32[]{:S(2)}) %collective-permute-start.4) | collective-permute-done | bytes 524320 | tf_op jit(solution)/shard_map/ppermute | solution.py:476
  52.7 10.4 %collective-permute-done.5.far_high = bf16[16,128,128]{2,1,0:T(8,128)(2,1)} collective-permute-done((bf16[16,128,128]{2,1,0:T(8,128)(2,1)}, bf16[16,128,128]{2,1,0:T(8,128)(2,1)}, u32[]{:S(2)}, u32[]{:S(2)}) %collective-permute-start.5) | collective-permute-done | bytes 524320 | tf_op jit(solution)/shard_map/ppermute | solution.py:477
  63.1 6.1 %shard_map.41 = bf16[160,128,128]{2,1,0:T(8,128)(2,1)} custom-call(s32[32,128]{1,0:T(8,128)} %get-tuple-element.37.table, bf16[96,128,128]{2,1,0:T(8,128)(2,1)} %bitcast.11, bf16[10,128,128]{2,1,0:T(8,128)(2,1)} %get-tuple-element.39.left_low, bf16[10,128,128]{2,1,0:T(8,128)(2,1)} %get-tuple-element.41.left_high, ...), custom_call_target="tpu_custom_call", output_to_operand_aliasing={{}: (12, {})} | custom-call | flops 2013265920 | bytes 13107200 | tf_op jit(solution)/shard_map/pallas_call | solution.py:524
  (1 shorter events, 0.0 us)
Async XLA Ops:
  1.5 25.6 %collective-permute-start.2 = (bf16[24,128,128]{2,1,0:T(8,128)(2,1)S(1)}, bf16[24,128,128]{2,1,0:T(8,128)(2,1)}, u32[]{:S(2)}, u32[]{:S(2)}) collective-permute-start(bf16[24,128,128]{2,1,0:T(8,128)(2,1)S(1)} %bitcast.13), channel_id=1, source_target_pairs={{0,1},{1,2},{2,3},{3,4},{4,5},{5,6},{6,7},{7,8},{8,9},{9,10},{10,1... | collective-permute-start | bytes 2359304 | tf_op jit(solution)/shard_map/ppermute | solution.py:438
  4.6 38.0 %collective-permute-start.3 = (bf16[24,128,128]{2,1,0:T(8,128)(2,1)S(1)}, bf16[24,128,128]{2,1,0:T(8,128)(2,1)}, u32[]{:S(2)}, u32[]{:S(2)}) collective-permute-start(bf16[24,128,128]{2,1,0:T(8,128)(2,1)S(1)} %bitcast.12), channel_id=1, source_target_pairs={{1,0},{2,1},{3,2},{4,3},{5,4},{6,5},{7,6},{8,7},{9,8},{10,9},{11,1... | collective-permute-start | bytes 2359304 | tf_op jit(solution)/shard_map/ppermute | solution.py:439
  15.9 36.8 %collective-permute-start.4 = (bf16[16,128,128]{2,1,0:T(8,128)(2,1)}, bf16[16,128,128]{2,1,0:T(8,128)(2,1)}, u32[]{:S(2)}, u32[]{:S(2)}) collective-permute-start(bf16[16,128,128]{2,1,0:T(8,128)(2,1)} %get-tuple-element.42), channel_id=1, source_target_pairs={{0,1},{1,2},{2,3},{3,4},{4,5},{5,6},{6,7},{7,8},{8,9},{9,10},{10,1... | collective-permute-start | bytes 1572872 | tf_op jit(solution)/shard_map/ppermute | solution.py:476
  15.9 47.1 %collective-permute-start.5 = (bf16[16,128,128]{2,1,0:T(8,128)(2,1)}, bf16[16,128,128]{2,1,0:T(8,128)(2,1)}, u32[]{:S(2)}, u32[]{:S(2)}) collective-permute-start(bf16[16,128,128]{2,1,0:T(8,128)(2,1)} %get-tuple-element.43), channel_id=1, source_target_pairs={{1,0},{2,1},{3,2},{4,3},{5,4},{6,5},{7,6},{8,7},{9,8},{10,9},{11,1... | collective-permute-start | bytes 1572872 | tf_op jit(solution)/shard_map/ppermute | solution.py:477

commit v5 on v4

--- a/solution.py
+++ b/solution.py
@@ -393,8 +393,7 @@
     half = BAND // 2
     outgoing = halo_terms(False, range(BAND))
     finish(late[4:])
-    outgoing += halo_terms(True, range(half, BAND))
-    outgoing += halo_terms(True, range(half))
+    outgoing += halo_terms(True, range(BAND))
     finish(outgoing)
 
 
@@ -483,7 +482,9 @@
         return pl.pallas_call(
             partial(near_kernel, dims, scale, upper),
             out_shape=[
-                shaped(rows * pnz), shaped(half_edge), shaped(half_edge), shaped(remaining),
+                shaped(rows * pnz), shaped(half_edge, jnp.float32),
+                shaped(half_edge, jnp.float32),
+                shaped(remaining),
                 shaped(lefts_count),
             ],
             in_specs=[hbm] * (4 + len(made)),
@@ -494,8 +495,8 @@
                 scratch(padded * nnz + 1),
                 scratch(rows * pnz + 1),
                 scratch((rows // 2 - BAND) * pnz),
-                scratch(half_edge),
-                scratch(half_edge),
+                scratch(half_edge, jnp.float32),
+                scratch(half_edge, jnp.float32),
                 pltpu.SMEM((32,), jnp.int32),
                 pltpu.SemaphoreType.DMA((1,)),
                 pltpu.SemaphoreType.DMA((3,)),
@@ -532,8 +533,8 @@
             scratch(padded * nnz + 1),
             scratch(2 * most + 1),
             scratch(edge + 1),
-            scratch(edge),
-            scratch(edge),
+            scratch(edge, jnp.float32),
+            scratch(edge, jnp.float32),
             scratch(edge),
             pltpu.SemaphoreType.DMA((1,)),
             pltpu.SemaphoreType.DMA((14 + 2 * BAND,)),

time: 69.9 us -> 70.9 us (1.014)
  Pallas kernels: 32.9 us -> 33.9 us
    pallas_call x1, Pallas kernels: 6.13 us -> 7.12 us  [body(): pl.pallas_call(partial(far_kernel, dims, scale), out_shape=shaped(rows *...]
  transfers between devices with their start and end apart: 4 -> 4, of which waited for: 3 -> 3; matrix products, arithmetic and copies ran while one was open for 2% -> 2% of each run, Pallas kernels for 39% -> 38%
where the time goes in v5:
time: 70.9 us; the launch traced here: 70.2 us
  Pallas kernels  33.9 us (48%)
  waiting for transfers between devices  17.8 us (25%)
  starting transfers between devices  10.1 us (14%)
  blocking collectives  4.89 us (7%)
  local copies, waits for them, and re-layouts  2.82 us (4%)
  between operations  0.71 us (1%)
    pallas_call x2, Pallas kernels, half_of_rows(): pl.pallas_call(partial(near_kernel, dims, scale, upper), out_shape=[shape...  18 us
    ppermute x1, waiting for transfers between devices, body(): far_high = lax.ppermute(down, AXES, backward)  10.4 us
    pallas_call x1, Pallas kernels, body(): pl.pallas_call(partial(far_kernel, dims, scale), out_shape=shaped(rows *...  7.12 us
    pallas_call x1, Pallas kernels, body(): pl.pallas_call(partial(inner_kernel, dims, scale), out_shape=[shaped((row...  6.91 us
    ppermute x1, waiting for transfers between devices, body(): high = lax.ppermute(x[:near], AXES, backward)  6.36 us
    pmax x1, blocking collectives, body(): largest = lax.pmax(largest[0, 0], 'groups')  4.89 us
    ppermute x1, starting transfers between devices, body(): far_high = lax.ppermute(down, AXES, backward)  4.43 us
    ppermute x1, starting transfers between devices, body(): low = lax.ppermute(x[rows * nnz - near:], AXES, forward)  3.08 us
  transfers between devices with their start and end apart: 4, of which 3 were waited for; matrix products, arithmetic and copies ran while one was open for 2% of the time, Pallas kernels for 38%

profile of v5, /device:TPU:0, one launch (start us, length us, event | category | flops | bytes accessed | tf_op | source)
XLA Modules:
  0.0 70.2 jit_solution(5224940869634066902)
XLA Ops:
  0.0 1.5 %fusion = (bf16[4,6,128,128]{3,2,1,0:T(8,128)(2,1)S(1)}, bf16[4,6,128,128]{3,2,1,0:T(8,128)(2,1)S(1)}) fusion(bf16[16,6,128,128]{3,2,1,0:T(8,128)(2,1)} %param.5), kind=kLoop, calls=%fused_computation | loop fusion | bytes 3145728 | tf_op jit(solution)/shard_map/slice | solution.py:438
  1.5 3.1 %collective-permute-start.2 = (bf16[24,128,128]{2,1,0:T(8,128)(2,1)S(1)}, bf16[24,128,128]{2,1,0:T(8,128)(2,1)}, u32[]{:S(2)}, u32[]{:S(2)}) collective-permute-start(bf16[24,128,128]{2,1,0:T(8,128)(2,1)S(1)} %bitcast.13), channel_id=1, source_target_pairs={{0,1},{1,2},{2,3},{3,4},{4,5},{5,6},{6,7},{7,8},{8,9},{9,10},{10,1... | collective-permute-start | bytes 2359304 | tf_op jit(solution)/shard_map/ppermute | solution.py:437
  4.6 2.5 %collective-permute-start.3 = (bf16[24,128,128]{2,1,0:T(8,128)(2,1)S(1)}, bf16[24,128,128]{2,1,0:T(8,128)(2,1)}, u32[]{:S(2)}, u32[]{:S(2)}) collective-permute-start(bf16[24,128,128]{2,1,0:T(8,128)(2,1)S(1)} %bitcast.12), channel_id=1, source_target_pairs={{1,0},{2,1},{3,2},{4,3},{5,4},{6,5},{7,6},{8,7},{9,8},{10,9},{11,1... | collective-permute-start | bytes 2359304 | tf_op jit(solution)/shard_map/ppermute | solution.py:438
  7.1 1.9 %shard_map.37 = (s32[32,128]{1,0:T(8,128)}, s32[8,128]{1,0:T(8,128)}) custom-call(s32[1]{0:T(128)} %bitcast.me, s32[6,256]{1,0:T(8,128)} %bitcast.15, s32[10,256]{1,0:T(8,128)} %bitcast.14), custom_call_target="tpu_custom_call" | custom-call | tf_op jit(solution)/shard_map/pallas_call | solution.py:441
  9.0 6.9 %shard_map.38 = (bf16[80,128,128]{2,1,0:T(8,128)(2,1)}, bf16[16,128,128]{2,1,0:T(8,128)(2,1)}, bf16[16,128,128]{2,1,0:T(8,128)(2,1)}) custom-call(s32[32,128]{1,0:T(8,128)} %get-tuple-element.37.table, bf16[96,128,128]{2,1,0:T(8,128)(2,1)} %bitcast.8), custom_call_target="tpu_custom_call" | custom-call | flops 2013265920 | bytes 6553600 | tf_op jit(solution)/shard_map/pallas_call | solution.py:456
  15.9 0.1 collective-permute-start.4
  16.0 4.4 %collective-permute-start.5 = (bf16[16,128,128]{2,1,0:T(8,128)(2,1)}, bf16[16,128,128]{2,1,0:T(8,128)(2,1)}, u32[]{:S(2)}, u32[]{:S(2)}) collective-permute-start(bf16[16,128,128]{2,1,0:T(8,128)(2,1)} %get-tuple-element.43), channel_id=1, source_target_pairs={{1,0},{2,1},{3,2},{4,3},{5,4},{6,5},{7,6},{8,7},{9,8},{10,9},{11,1... | collective-permute-start | bytes 1572872 | tf_op jit(solution)/shard_map/ppermute | solution.py:476
  20.4 1.3 %slice.19 = s32[1,1]{1,0:T(1,128)} slice(s32[8,128]{1,0:T(8,128)} %get-tuple-element.44), slice={[0:1], [0:1]} | slice | bytes 8 | tf_op jit(solution)/shard_map/slice | solution.py:451
  21.7 4.9 %pmax.7 = s32[]{:T(128)} all-reduce(s32[]{:T(128)} %bitcast.6), channel_id=1, replica_groups=mesh['groups'=2,'grid'=4,'rep'=4] {'groups'}, use_global_device_ids=true, to_apply=%region_0.0 | all-reduce | flops 1 | bytes 8 | tf_op jit(solution)/shard_map/pmax | solution.py:451
  27.2 0.0 collective-permute-done.2.near
  27.2 9.0 %shard_map.39 = (bf16[160,128,128]{2,1,0:T(8,128)(2,1)}, f32[40,128,128]{2,1,0:T(8,128)}, f32[40,128,128]{2,1,0:T(8,128)}, bf16[8,128,128]{2,1,0:T(8,128)(2,1)S(1)}, bf16[10,128,128]{2,1,0:T(8,128)(2,1)}) custom-call(s32[32,128]{1,0:T(8,128)} %get-tuple-element.37.table, bf16[96,128,128]{2,1,0:T(8,128)(2,1)} %bitcast.9, ...), custom_call_target="tpu_custom_call" | custom-call | flops 4026531840 | bytes 16384000 | tf_op jit(solution)/shard_map/pallas_call | solution.py:482
  36.2 6.4 %collective-permute-done.3.near = bf16[24,128,128]{2,1,0:T(8,128)(2,1)} collective-permute-done((bf16[24,128,128]{2,1,0:T(8,128)(2,1)S(1)}, bf16[24,128,128]{2,1,0:T(8,128)(2,1)}, u32[]{:S(2)}, u32[]{:S(2)}) %collective-permute-start.3) | collective-permute-done | bytes 786464 | tf_op jit(solution)/shard_map/ppermute | solution.py:438
  42.6 9.0 %shard_map.40 = (bf16[160,128,128]{2,1,0:T(8,128)(2,1)}, f32[40,128,128]{2,1,0:T(8,128)}, f32[40,128,128]{2,1,0:T(8,128)}, bf16[8,128,128]{2,1,0:T(8,128)(2,1)S(1)}, bf16[10,128,128]{2,1,0:T(8,128)(2,1)}) custom-call(s32[32,128]{1,0:T(8,128)} %get-tuple-element.37.table, bf16[96,128,128]{2,1,0:T(8,128)(2,1)} %bitcast.10, ...), custom_call_target="tpu_custom_call", output_to_operand_aliasing={{0}: (4, {})} | custom-call | flops 4026531840 | bytes 16384000 | tf_op jit(solution)/shard_map/pallas_call | solution.py:482
  51.6 1.1 %collective-permute-done.4.far_low = bf16[16,128,128]{2,1,0:T(8,128)(2,1)} collective-permute-done((bf16[16,128,128]{2,1,0:T(8,128)(2,1)}, bf16[16,128,128]{2,1,0:T(8,128)(2,1)}, u32[]{:S(2)}, u32[]{:S(2)}) %collective-permute-start.4) | collective-permute-done | bytes 524320 | tf_op jit(solution)/shard_map/ppermute | solution.py:475
  52.7 10.4 %collective-permute-done.5.far_high = bf16[16,128,128]{2,1,0:T(8,128)(2,1)} collective-permute-done((bf16[16,128,128]{2,1,0:T(8,128)(2,1)}, bf16[16,128,128]{2,1,0:T(8,128)(2,1)}, u32[]{:S(2)}, u32[]{:S(2)}) %collective-permute-start.5) | collective-permute-done | bytes 524320 | tf_op jit(solution)/shard_map/ppermute | solution.py:476
  63.1 7.1 %shard_map.41 = bf16[160,128,128]{2,1,0:T(8,128)(2,1)} custom-call(s32[32,128]{1,0:T(8,128)} %get-tuple-element.37.table, bf16[96,128,128]{2,1,0:T(8,128)(2,1)} %bitcast.11, bf16[10,128,128]{2,1,0:T(8,128)(2,1)} %get-tuple-element.39.left_low, bf16[10,128,128]{2,1,0:T(8,128)(2,1)} %get-tuple-element.41.left_high, ...), custom_call_target="tpu_custom_call", output_to_operand_aliasing={{}: (12, {})} | custom-call | flops 2013265920 | bytes 13107200 | tf_op jit(solution)/shard_map/pallas_call | solution.py:525
  (1 shorter events, 0.0 us)
Async XLA Ops:
  1.5 25.7 %collective-permute-start.2 = (bf16[24,128,128]{2,1,0:T(8,128)(2,1)S(1)}, bf16[24,128,128]{2,1,0:T(8,128)(2,1)}, u32[]{:S(2)}, u32[]{:S(2)}) collective-permute-start(bf16[24,128,128]{2,1,0:T(8,128)(2,1)S(1)} %bitcast.13), channel_id=1, source_target_pairs={{0,1},{1,2},{2,3},{3,4},{4,5},{5,6},{6,7},{7,8},{8,9},{9,10},{10,1... | collective-permute-start | bytes 2359304 | tf_op jit(solution)/shard_map/ppermute | solution.py:437
  4.6 38.0 %collective-permute-start.3 = (bf16[24,128,128]{2,1,0:T(8,128)(2,1)S(1)}, bf16[24,128,128]{2,1,0:T(8,128)(2,1)}, u32[]{:S(2)}, u32[]{:S(2)}) collective-permute-start(bf16[24,128,128]{2,1,0:T(8,128)(2,1)S(1)} %bitcast.12), channel_id=1, source_target_pairs={{1,0},{2,1},{3,2},{4,3},{5,4},{6,5},{7,6},{8,7},{9,8},{10,9},{11,1... | collective-permute-start | bytes 2359304 | tf_op jit(solution)/shard_map/ppermute | solution.py:438
  15.9 36.8 %collective-permute-start.4 = (bf16[16,128,128]{2,1,0:T(8,128)(2,1)}, bf16[16,128,128]{2,1,0:T(8,128)(2,1)}, u32[]{:S(2)}, u32[]{:S(2)}) collective-permute-start(bf16[16,128,128]{2,1,0:T(8,128)(2,1)} %get-tuple-element.42), channel_id=1, source_target_pairs={{0,1},{1,2},{2,3},{3,4},{4,5},{5,6},{6,7},{7,8},{8,9},{9,10},{10,1... | collective-permute-start | bytes 1572872 | tf_op jit(solution)/shard_map/ppermute | solution.py:475
  16.0 47.1 %collective-permute-start.5 = (bf16[16,128,128]{2,1,0:T(8,128)(2,1)}, bf16[16,128,128]{2,1,0:T(8,128)(2,1)}, u32[]{:S(2)}, u32[]{:S(2)}) collective-permute-start(bf16[16,128,128]{2,1,0:T(8,128)(2,1)} %get-tuple-element.43), channel_id=1, source_target_pairs={{1,0},{2,1},{3,2},{4,3},{5,4},{6,5},{7,6},{8,7},{9,8},{10,9},{11,1... | collective-permute-start | bytes 1572872 | tf_op jit(solution)/shard_map/ppermute | solution.py:476

commit v6 on v5

--- a/solution.py
+++ b/solution.py
@@ -330,7 +330,7 @@
 
 def far_kernel(
     dims, scale, table, x, left_low, left_high, far_low, far_high, more_low, more_high, gram_low, gram_high,
-    part_low, part_high, unused, out, ints, pool, far, gram, near_sums, own_sums, done, table_sem,
+    part_low, part_high, unused, out, ints, pool, left, far, gram, near_sums, own_sums, done, table_sem,
     sems
 ):
     rows, nnz, pnz = dims
@@ -341,11 +341,7 @@
         (far_low, far, 0), (more_low, far, first),
         (far_high, far, near), (more_high, far, near + first),
     ]
-    for upper, lefts in ((False, left_low), (True, left_high)):
-        place = 0
-        for row, slot, many in crossing(dims, upper)[:BAND]:
-            moves.append((lefts.at[pl.ds(place, many)], pool, (REACH + row) * nnz + slot))
-            place += many
+    moves += [(left_low, left, 0), (left_high, left, left_low.shape[0])]
     early = [table_copy(table, ints, table_sem)] + begin(sems, moves)
     late = begin(sems.at[pl.ds(len(moves), 6)], [
         (gram_low, near_sums, 0), (gram_high, near_sums, edge),
@@ -359,9 +355,12 @@
     finish(early)
 
     def far_terms(upper):
+        place = left_low.shape[0] if upper else 0
         for e, (row, slot, many) in enumerate(crossing(dims, upper)[:BAND]):
             slots = range(slot, slot + many)
-            blocks = products(dims, ints, REACH + row, slots, TO_FAR, pool, far)
+            base = (REACH + row) * nnz + slot - place
+            place += many
+            blocks = products(dims, ints, REACH + row, slots, TO_FAR, left, far, base)
             for p, block in enumerate(blocks):
                 n = (upper * BAND + e) * pnz + p
                 whole = near_sums[n].astype(jnp.float32) + block
@@ -393,7 +392,8 @@
     half = BAND // 2
     outgoing = halo_terms(False, range(BAND))
     finish(late[4:])
-    outgoing += halo_terms(True, range(BAND))
+    outgoing += halo_terms(True, range(half, BAND))
+    outgoing += halo_terms(True, range(half))
     finish(outgoing)
 
 
@@ -531,6 +531,7 @@
         scratch_shapes=[
             table,
             scratch(padded * nnz + 1),
+            scratch(2 * lefts_count),
             scratch(2 * most + 1),
             scratch(edge + 1),
             scratch(edge, jnp.float32),

time: 70.9 us -> 70.7 us (level)
  no operation moved by 1% of the time
where the time goes in v6:
time: 70.7 us; the launch traced here: 69.9 us
  Pallas kernels  33.6 us (48%)
  waiting for transfers between devices  17.8 us (25%)
  starting transfers between devices  10.1 us (14%)
  blocking collectives  4.89 us (7%)
  local copies, waits for them, and re-layouts  2.82 us (4%)
  between operations  0.71 us (1%)
    pallas_call x2, Pallas kernels, half_of_rows(): pl.pallas_call(partial(near_kernel, dims, scale, upper), out_shape=[shape...  18 us
    ppermute x1, waiting for transfers between devices, body(): far_high = lax.ppermute(down, AXES, backward)  10.4 us
    pallas_call x1, Pallas kernels, body(): pl.pallas_call(partial(inner_kernel, dims, scale), out_shape=[shaped((row...  6.91 us
    pallas_call x1, Pallas kernels, body(): pl.pallas_call(partial(far_kernel, dims, scale), out_shape=shaped(rows *...  6.88 us
    ppermute x1, waiting for transfers between devices, body(): high = lax.ppermute(x[:near], AXES, backward)  6.36 us
    pmax x1, blocking collectives, body(): largest = lax.pmax(largest[0, 0], 'groups')  4.89 us
    ppermute x1, starting transfers between devices, body(): far_high = lax.ppermute(down, AXES, backward)  4.43 us
    ppermute x1, starting transfers between devices, body(): low = lax.ppermute(x[rows * nnz - near:], AXES, forward)  3.08 us
  transfers between devices with their start and end apart: 4, of which 3 were waited for; matrix products, arithmetic and copies ran while one was open for 2% of the time, Pallas kernels for 38%

profile of v6, /device:TPU:0, one launch (start us, length us, event | category | flops | bytes accessed | tf_op | source)
XLA Modules:
  0.0 69.9 jit_solution(5288282874112272809)
XLA Ops:
  0.0 1.5 %fusion = (bf16[4,6,128,128]{3,2,1,0:T(8,128)(2,1)S(1)}, bf16[4,6,128,128]{3,2,1,0:T(8,128)(2,1)S(1)}) fusion(bf16[16,6,128,128]{3,2,1,0:T(8,128)(2,1)} %param.5), kind=kLoop, calls=%fused_computation | loop fusion | bytes 3145728 | tf_op jit(solution)/shard_map/slice | solution.py:438
  1.5 3.1 %collective-permute-start.2 = (bf16[24,128,128]{2,1,0:T(8,128)(2,1)S(1)}, bf16[24,128,128]{2,1,0:T(8,128)(2,1)}, u32[]{:S(2)}, u32[]{:S(2)}) collective-permute-start(bf16[24,128,128]{2,1,0:T(8,128)(2,1)S(1)} %bitcast.13), channel_id=1, source_target_pairs={{0,1},{1,2},{2,3},{3,4},{4,5},{5,6},{6,7},{7,8},{8,9},{9,10},{10,1... | collective-permute-start | bytes 2359304 | tf_op jit(solution)/shard_map/ppermute | solution.py:437
  4.6 2.5 %collective-permute-start.3 = (bf16[24,128,128]{2,1,0:T(8,128)(2,1)S(1)}, bf16[24,128,128]{2,1,0:T(8,128)(2,1)}, u32[]{:S(2)}, u32[]{:S(2)}) collective-permute-start(bf16[24,128,128]{2,1,0:T(8,128)(2,1)S(1)} %bitcast.12), channel_id=1, source_target_pairs={{1,0},{2,1},{3,2},{4,3},{5,4},{6,5},{7,6},{8,7},{9,8},{10,9},{11,1... | collective-permute-start | bytes 2359304 | tf_op jit(solution)/shard_map/ppermute | solution.py:438
  7.1 1.9 %shard_map.37 = (s32[32,128]{1,0:T(8,128)}, s32[8,128]{1,0:T(8,128)}) custom-call(s32[1]{0:T(128)} %bitcast.me, s32[6,256]{1,0:T(8,128)} %bitcast.15, s32[10,256]{1,0:T(8,128)} %bitcast.14), custom_call_target="tpu_custom_call" | custom-call | tf_op jit(solution)/shard_map/pallas_call | solution.py:441
  9.0 6.9 %shard_map.38 = (bf16[80,128,128]{2,1,0:T(8,128)(2,1)}, bf16[16,128,128]{2,1,0:T(8,128)(2,1)}, bf16[16,128,128]{2,1,0:T(8,128)(2,1)}) custom-call(s32[32,128]{1,0:T(8,128)} %get-tuple-element.37.table, bf16[96,128,128]{2,1,0:T(8,128)(2,1)} %bitcast.8), custom_call_target="tpu_custom_call" | custom-call | flops 2013265920 | bytes 6553600 | tf_op jit(solution)/shard_map/pallas_call | solution.py:456
  15.9 0.1 collective-permute-start.4
  16.0 4.4 %collective-permute-start.5 = (bf16[16,128,128]{2,1,0:T(8,128)(2,1)}, bf16[16,128,128]{2,1,0:T(8,128)(2,1)}, u32[]{:S(2)}, u32[]{:S(2)}) collective-permute-start(bf16[16,128,128]{2,1,0:T(8,128)(2,1)} %get-tuple-element.43), channel_id=1, source_target_pairs={{1,0},{2,1},{3,2},{4,3},{5,4},{6,5},{7,6},{8,7},{9,8},{10,9},{11,1... | collective-permute-start | bytes 1572872 | tf_op jit(solution)/shard_map/ppermute | solution.py:476
  20.4 1.3 %slice.19 = s32[1,1]{1,0:T(1,128)} slice(s32[8,128]{1,0:T(8,128)} %get-tuple-element.44), slice={[0:1], [0:1]} | slice | bytes 8 | tf_op jit(solution)/shard_map/slice | solution.py:451
  21.7 4.9 %pmax.7 = s32[]{:T(128)} all-reduce(s32[]{:T(128)} %bitcast.6), channel_id=1, replica_groups=mesh['groups'=2,'grid'=4,'rep'=4] {'groups'}, use_global_device_ids=true, to_apply=%region_0.0 | all-reduce | flops 1 | bytes 8 | tf_op jit(solution)/shard_map/pmax | solution.py:451
  27.2 0.0 collective-permute-done.2.near
  27.2 9.0 %shard_map.39 = (bf16[160,128,128]{2,1,0:T(8,128)(2,1)}, f32[40,128,128]{2,1,0:T(8,128)}, f32[40,128,128]{2,1,0:T(8,128)}, bf16[8,128,128]{2,1,0:T(8,128)(2,1)S(1)}, bf16[10,128,128]{2,1,0:T(8,128)(2,1)}) custom-call(s32[32,128]{1,0:T(8,128)} %get-tuple-element.37.table, bf16[96,128,128]{2,1,0:T(8,128)(2,1)} %bitcast.9, ...), custom_call_target="tpu_custom_call" | custom-call | flops 4026531840 | bytes 16384000 | tf_op jit(solution)/shard_map/pallas_call | solution.py:482
  36.2 6.4 %collective-permute-done.3.near = bf16[24,128,128]{2,1,0:T(8,128)(2,1)} collective-permute-done((bf16[24,128,128]{2,1,0:T(8,128)(2,1)S(1)}, bf16[24,128,128]{2,1,0:T(8,128)(2,1)}, u32[]{:S(2)}, u32[]{:S(2)}) %collective-permute-start.3) | collective-permute-done | bytes 786464 | tf_op jit(solution)/shard_map/ppermute | solution.py:438
  42.6 9.0 %shard_map.40 = (bf16[160,128,128]{2,1,0:T(8,128)(2,1)}, f32[40,128,128]{2,1,0:T(8,128)}, f32[40,128,128]{2,1,0:T(8,128)}, bf16[8,128,128]{2,1,0:T(8,128)(2,1)S(1)}, bf16[10,128,128]{2,1,0:T(8,128)(2,1)}) custom-call(s32[32,128]{1,0:T(8,128)} %get-tuple-element.37.table, bf16[96,128,128]{2,1,0:T(8,128)(2,1)} %bitcast.10, ...), custom_call_target="tpu_custom_call", output_to_operand_aliasing={{0}: (4, {})} | custom-call | flops 4026531840 | bytes 16384000 | tf_op jit(solution)/shard_map/pallas_call | solution.py:482
  51.6 1.1 %collective-permute-done.4.far_low = bf16[16,128,128]{2,1,0:T(8,128)(2,1)} collective-permute-done((bf16[16,128,128]{2,1,0:T(8,128)(2,1)}, bf16[16,128,128]{2,1,0:T(8,128)(2,1)}, u32[]{:S(2)}, u32[]{:S(2)}) %collective-permute-start.4) | collective-permute-done | bytes 524320 | tf_op jit(solution)/shard_map/ppermute | solution.py:475
  52.7 10.4 %collective-permute-done.5.far_high = bf16[16,128,128]{2,1,0:T(8,128)(2,1)} collective-permute-done((bf16[16,128,128]{2,1,0:T(8,128)(2,1)}, bf16[16,128,128]{2,1,0:T(8,128)(2,1)}, u32[]{:S(2)}, u32[]{:S(2)}) %collective-permute-start.5) | collective-permute-done | bytes 524320 | tf_op jit(solution)/shard_map/ppermute | solution.py:476
  63.1 6.9 %shard_map.41 = bf16[160,128,128]{2,1,0:T(8,128)(2,1)} custom-call(s32[32,128]{1,0:T(8,128)} %get-tuple-element.37.table, bf16[96,128,128]{2,1,0:T(8,128)(2,1)} %bitcast.11, bf16[10,128,128]{2,1,0:T(8,128)(2,1)} %get-tuple-element.39.left_low, bf16[10,128,128]{2,1,0:T(8,128)(2,1)} %get-tuple-element.41.left_high, ...), custom_call_target="tpu_custom_call", output_to_operand_aliasing={{}: (12, {})} | custom-call | flops 2013265920 | bytes 13107200 | tf_op jit(solution)/shard_map/pallas_call | solution.py:525
  (1 shorter events, 0.0 us)
Async XLA Ops:
  1.5 25.7 %collective-permute-start.2 = (bf16[24,128,128]{2,1,0:T(8,128)(2,1)S(1)}, bf16[24,128,128]{2,1,0:T(8,128)(2,1)}, u32[]{:S(2)}, u32[]{:S(2)}) collective-permute-start(bf16[24,128,128]{2,1,0:T(8,128)(2,1)S(1)} %bitcast.13), channel_id=1, source_target_pairs={{0,1},{1,2},{2,3},{3,4},{4,5},{5,6},{6,7},{7,8},{8,9},{9,10},{10,1... | collective-permute-start | bytes 2359304 | tf_op jit(solution)/shard_map/ppermute | solution.py:437
  4.6 38.0 %collective-permute-start.3 = (bf16[24,128,128]{2,1,0:T(8,128)(2,1)S(1)}, bf16[24,128,128]{2,1,0:T(8,128)(2,1)}, u32[]{:S(2)}, u32[]{:S(2)}) collective-permute-start(bf16[24,128,128]{2,1,0:T(8,128)(2,1)S(1)} %bitcast.12), channel_id=1, source_target_pairs={{1,0},{2,1},{3,2},{4,3},{5,4},{6,5},{7,6},{8,7},{9,8},{10,9},{11,1... | collective-permute-start | bytes 2359304 | tf_op jit(solution)/shard_map/ppermute | solution.py:438
  15.9 36.8 %collective-permute-start.4 = (bf16[16,128,128]{2,1,0:T(8,128)(2,1)}, bf16[16,128,128]{2,1,0:T(8,128)(2,1)}, u32[]{:S(2)}, u32[]{:S(2)}) collective-permute-start(bf16[16,128,128]{2,1,0:T(8,128)(2,1)} %get-tuple-element.42), channel_id=1, source_target_pairs={{0,1},{1,2},{2,3},{3,4},{4,5},{5,6},{6,7},{7,8},{8,9},{9,10},{10,1... | collective-permute-start | bytes 1572872 | tf_op jit(solution)/shard_map/ppermute | solution.py:475
  16.0 47.1 %collective-permute-start.5 = (bf16[16,128,128]{2,1,0:T(8,128)(2,1)}, bf16[16,128,128]{2,1,0:T(8,128)(2,1)}, u32[]{:S(2)}, u32[]{:S(2)}) collective-permute-start(bf16[16,128,128]{2,1,0:T(8,128)(2,1)} %get-tuple-element.43), channel_id=1, source_target_pairs={{1,0},{2,1},{3,2},{4,3},{5,4},{6,5},{7,6},{8,7},{9,8},{10,9},{11,1... | collective-permute-start | bytes 1572872 | tf_op jit(solution)/shard_map/ppermute | solution.py:476
